TPU v7x, 32 devices: a whole 2x2x4 slice. The times are simulated.
32 devices in a mesh: groups: 2 (over y), ctx: 4 (over x, core), head: 4 (over z).
Axes of the slice: x: 2, y: 2, z: 4, core: 2. Of those that a mesh axis runs over, the one named last changes fastest.
Arguments:
- queries: bfloat16 [384, 64, 128], P(('groups', 'ctx'), 'head'), parts along dimension 0, may hold values from -16 to 16
- prefix_keys: bfloat16 [16384, 8, 128], P(('groups', 'ctx'), 'head'), parts along dimension 0, may hold values from -16 to 16
- prefix_values: bfloat16 [16384, 8, 128], P(('groups', 'ctx'), 'head'), parts along dimension 0, may hold values from -12 to 12
- suffix_keys: bfloat16 [384, 512, 8, 128], P(('groups', 'ctx'), None, 'head'), parts along dimension 0, may hold values from -16 to 16
- suffix_values: bfloat16 [384, 512, 8, 128], P(('groups', 'ctx'), None, 'head'), parts along dimension 0, may hold values from -12 to 12
- lengths: int32 [384], P(('groups', 'ctx')), parts along dimension 0, may hold values from 1 to 512, as said below
Outputs:
- attended: bfloat16 [384, 64, 128], P(('groups', 'ctx'), 'head'), parts along dimension 0
There are 2 independent parts, one for each index of `groups`. A program takes and returns all parts, laid end to end along the dimension named above; each array names one. Nothing has to cross between parts.
Inputs may be any that keep to these rules, and one draw needn't show every extreme that they name: The live slots of a row are its first lengths[r] slots; some row of each part has exactly 512.
All inputs are finite; a program needn't handle non-finite values.
Results may differ from a plain program's by a relative error of at most 0.0025.
Values may be sent and summed in bfloat16 or wider, within the bound.
No kernel may reach another device: no remote copies, remote signals or barrier semaphores. Data moves between devices by JAX's collectives and lax.ppermute only.
A program may use at most 128 MiB of HBM per device.

v0:
```python
from functools import partial

import jax
import jax.numpy as jnp
from jax import lax
from jax.experimental import pallas as pl
from jax.experimental.pallas import tpu as pltpu
from jax.sharding import PartitionSpec as P

LOG2E = 1.4426950408889634
F32 = jnp.float32
BF16 = jnp.bfloat16
VMEM = pl.BlockSpec(memory_space=pltpu.VMEM)


def split_heads(q_ref, kv_heads):
    rows, heads, d = q_ref.shape
    group = heads // kv_heads
    wide = q_ref[...].astype(F32)
    return [
        wide[:, h * group : (h + 1) * group, :].reshape(rows * group, d).astype(BF16)
        for h in range(kv_heads)
    ]


def scores_of(q, k):
    return lax.dot_general(q, k, (((1,), (1,)), ((), ())), preferred_element_type=F32)


def attend_blocks(heads_q, kv_refs, c):
    d = heads_q[0].shape[1]
    blocks = len(kv_refs) // 2
    items = [(h, b) for h in range(len(heads_q)) for b in range(blocks)]
    parts = {}
    s = w = None
    for step in range(len(items) + 2):
        s_next = w_next = None
        if step < len(items):
            h, b = items[step]
            s_next = scores_of(heads_q[h], kv_refs[2 * b][h])
        if w is not None:
            h, b = items[step - 2]
            v = kv_refs[2 * b + 1][h]
            oa = jnp.dot(w[0], jnp.concatenate([v, jnp.ones_like(v)], axis=1), preferred_element_type=F32)
            parts[h, b] = (oa[:, :d], oa[:, d:], w[1])
        if s is not None:
            top = jnp.max(s, axis=1, keepdims=True)
            w_next = (jnp.exp2(s * c - top * c).astype(BF16), top * c)
        s, w = s_next, w_next
    results = []
    for h in range(len(heads_q)):
        top = parts[h, 0][2]
        for b in range(1, blocks):
            top = jnp.maximum(top, parts[h, b][2])
        acc = 0.0
        total = 0.0
        for b in range(blocks):
            o, l, t = parts[h, b]
            scale = jnp.exp2(t - top)
            acc = acc + o * scale
            total = total + l * scale
        results.append((acc / total, top + jnp.log2(total)))
    return results


def lane_eye(n):
    return lax.broadcasted_iota(jnp.int32, (n, n), 0) == lax.broadcasted_iota(jnp.int32, (n, n), 1)


def other_kernel(q_ref, *refs, c, kv_heads, pieces):
    kv_refs, msg_ref = refs[:-1], refs[-1]
    heads_q = split_heads(q_ref, kv_heads)
    m, d = heads_q[0].shape
    eye = lane_eye(d)
    packed = []
    for h, (o, lse) in enumerate(attend_blocks(heads_q, kv_refs, c)):
        msg_ref[h * m : (h + 1) * m, :] = o.astype(BF16)
        packed.append(jnp.sum(jnp.where(eye, lse.reshape(m // d, d, d), 0.0), axis=1))
    rest = jnp.concatenate(packed, axis=0)
    out = []
    for _ in range(3):
        piece = rest.astype(BF16).astype(F32)
        out.append(piece)
        rest = rest - piece
    used = 3 * out[0].shape[0]
    if pieces > used:
        out.append(jnp.zeros((pieces - used, d), F32))
    msg_ref[kv_heads * m :, :] = jnp.concatenate(out, axis=0).astype(BF16)


def own_kernel(q_ref, *refs, c, kv_heads, blocks):
    kv_refs, before, (o_ref, lse_ref) = refs[: 2 * blocks], refs[2 * blocks : -2], refs[-2:]
    heads_q = [q_ref[h] for h in range(kv_heads)]
    for h, (o, lse) in enumerate(attend_blocks(heads_q, kv_refs, c)):
        if before:
            o_old, lse_old = before[0][h], before[1][h]
            top = jnp.maximum(lse, lse_old)
            new, old = jnp.exp2(lse - top), jnp.exp2(lse_old - top)
            total = new + old
            o = (o * new + o_old * old) / total
            lse = top + jnp.log2(total)
        o_ref[h] = o
        lse_ref[h] = jnp.broadcast_to(lse, o.shape)


def suffix_kernel(
    len_ref, q_ref, k_ref, v_ref, op_ref, lp_ref, o_ref, lse_ref, item_ref, oi_ref, li_ref, *, c, kv_heads, batch, chunk
):
    rows, heads, d = q_ref.shape
    group = heads // kv_heads
    width = chunk * kv_heads
    chunks = k_ref.shape[1] // width
    lane = lax.broadcasted_iota(jnp.int32, (heads, width), 1)
    head = lax.broadcasted_iota(jnp.int32, (heads, width), 0) // group
    place = jnp.where(lane % kv_heads == head, lane // kv_heads, chunk * chunks)

    def enlist(r, count):
        for j in range(chunks):
            item_ref[count + j] = r * chunks + j
        return count + (len_ref[r] + chunk - 1) // chunk

    count = lax.fori_loop(0, rows, enlist, 0)
    for j in range(2 * batch):
        item_ref[count + j] = 0
    batches = (count + batch - 1) // batch

    def part(slot):
        r = slot // chunks
        j = slot - r * chunks
        return r, j, pl.ds(pl.multiple_of(j * width, width), width)

    def score_batch(i):
        found = []
        for t in range(batch):
            r, _, span = part(item_ref[i * batch + t])
            found.append(scores_of(q_ref[r], k_ref[r, span, :]))
        return tuple(found)

    def body(i, scores):
        ahead = score_batch(i + 1)
        weights = []
        for t in range(batch):
            r, j, _ = part(item_ref[i * batch + t])
            s = jnp.where(place < len_ref[r] - j * chunk, scores[t], -jnp.inf)
            top = jnp.max(s, axis=1, keepdims=True)
            w = jnp.exp2(s * c - top * c).astype(BF16)
            weights.append((w, top * c, jnp.sum(w.astype(F32), axis=1, keepdims=True)))
        for t in range(batch):
            slot = item_ref[i * batch + t]
            r, _, span = part(slot)
            w, top, total = weights[t]
            o = jnp.dot(w, v_ref[r, span, :], preferred_element_type=F32)
            oi_ref[slot] = o * (1.0 / total)
            li_ref[slot] = jnp.broadcast_to(top + jnp.log2(total), (heads, d))
        return ahead

    lax.fori_loop(0, batches, body, score_batch(0))

    def merge(r, _):
        live = (len_ref[r] + chunk - 1) // chunk
        rows_of = pl.ds(pl.multiple_of(r * group, group), group)
        parts = [
            (
                jnp.concatenate([op_ref[h, rows_of, :] for h in range(kv_heads)], axis=0),
                jnp.concatenate([lp_ref[h, rows_of, :] for h in range(kv_heads)], axis=0),
            )
        ]
        for j in range(chunks):
            slot = r * chunks + j
            parts.append((jnp.where(j < live, oi_ref[slot], 0.0), jnp.where(j < live, li_ref[slot], -jnp.inf)))
        top = parts[0][1]
        for p in parts[1:]:
            top = jnp.maximum(top, p[1])
        acc = 0.0
        total = 0.0
        for o, l in parts:
            w = jnp.exp2(l - top)
            acc = acc + o * w
            total = total + w
        o_ref[r] = acc / total
        lse_ref[r] = top + jnp.log2(total)
        return 0

    lax.fori_loop(0, rows, merge, 0, unroll=16 if rows % 16 == 0 else 1)


def merge_kernel(os_ref, ls_ref, *refs, kv_heads, group):
    msg_refs, out_ref = refs[:-1], refs[-1]
    rows, heads, d = os_ref.shape
    m = rows * group
    n = m // d
    eye = lane_eye(d)
    results = []
    for h in range(kv_heads):
        cols = slice(h * group, (h + 1) * group)
        parts = [(os_ref[:, cols, :].reshape(m, d), ls_ref[:, cols, :].reshape(m, d))]
        for msg in msg_refs:
            o = msg[h * m : (h + 1) * m, :].astype(F32)
            tail = msg[kv_heads * m :, :].astype(F32)
            lse = sum(tail[(p * kv_heads + h) * n : (p * kv_heads + h + 1) * n] for p in range(3))
            lse = jnp.where(eye, jnp.broadcast_to(lse[:, None, :], (n, d, d)), 0.0)
            lse = jnp.sum(lse, axis=2, keepdims=True).reshape(m, 1)
            parts.append((o, jnp.broadcast_to(lse, (m, d))))
        top = parts[0][1]
        for part in parts[1:]:
            top = jnp.maximum(top, part[1])
        acc = 0.0
        total = 0.0
        for o, l in parts:
            w = jnp.exp2(l - top)
            acc = acc + o * w
            total = total + w
        results.append((acc / total).reshape(rows, group, d))
    out_ref[...] = jnp.concatenate(results, axis=1).astype(BF16)


def shards(queries, prefix_keys, prefix_values, suffix_keys, suffix_values, lengths):
    rows, heads, d = queries.shape
    kv_heads = prefix_keys.shape[1]
    group = heads // kv_heads
    span = suffix_keys.shape[1]
    c = d ** (-0.5) * LOG2E
    n = lax.axis_size("ctx")
    cores = 2 if n % 2 == 0 else 1
    chips = n // cores
    m = rows * group
    pieces = -(-3 * kv_heads * (m // d) // 16) * 16

    def shift(x, by):
        return lax.ppermute(x, "ctx", [(i, (i + by) % n) for i in range(n)])

    def call(kernel, out_shape, operands, specs, scratch=(), mib=40, name=None, flops=0, moved=0):
        single = not isinstance(out_shape, tuple)
        return pl.pallas_call(
            kernel,
            out_shape=out_shape,
            in_specs=specs,
            out_specs=VMEM if single else (VMEM,) * len(out_shape),
            scratch_shapes=scratch,
            compiler_params=pltpu.CompilerParams(vmem_limit_bytes=mib << 20),
            cost_estimate=pl.CostEstimate(flops=flops, bytes_accessed=moved, transcendentals=0),
            name=name,
        )(*operands)

    raw = [prefix_keys.reshape(-1, d), prefix_values.reshape(-1, d)]
    split_queries = queries.reshape(rows, kv_heads, group, d).transpose(1, 0, 2, 3).reshape(kv_heads, m, d)

    def by_head(x):
        return x.reshape(-1, kv_heads, d).transpose(1, 0, 2)

    visiting = [shift(queries, j * cores) for j in range(1, chips)]

    spread = prefix_keys.shape[0]
    flops = 16 * m * kv_heads * spread * d
    moved = 4 * kv_heads * spread * d

    def own_rows(kv, before):
        operands = (split_queries, *kv, *before)
        return call(
            partial(own_kernel, c=c, kv_heads=kv_heads, blocks=len(kv) // 2),
            (jax.ShapeDtypeStruct((kv_heads, m, d), F32),) * 2,
            operands,
            [VMEM] * len(operands),
            mib=24,
            name="own",
            flops=flops,
            moved=moved,
        )

    flat = []
    own = ()
    if cores == 2:
        swap = [(i, i ^ 1) for i in range(n)]
        flat = [by_head(lax.ppermute(x, "ctx", swap)) for x in raw]
        own = own_rows(flat, ())
        raw, own = lax.optimization_barrier((raw, own))
    raw = [by_head(x) for x in raw]
    own_o, own_l = own_rows(raw, own)
    flat = [*flat, *raw]
    visiting, own_o, own_l = lax.optimization_barrier((visiting, own_o, own_l))
    message = jax.ShapeDtypeStruct((kv_heads * m + pieces, d), BF16)
    returned = []
    for j, q in enumerate(visiting):
        msg = call(
            partial(other_kernel, c=c, kv_heads=kv_heads, pieces=pieces),
            message,
            (q, *flat),
            [VMEM] * (1 + len(flat)),
            mib=24,
            name="visiting",
            flops=cores * flops,
            moved=cores * moved,
        )
        returned.append(shift(msg, -(j + 1) * cores))
    slots = span * kv_heads
    chunk = 128 if span % 128 == 0 else span
    batch = 16
    items = rows * (span // chunk)
    local = call(
        partial(suffix_kernel, c=c, kv_heads=kv_heads, batch=batch, chunk=chunk),
        (jax.ShapeDtypeStruct((rows, heads, d), F32),) * 2,
        (lengths, queries, suffix_keys.reshape(rows, slots, d), suffix_values.reshape(rows, slots, d), own_o, own_l),
        [pl.BlockSpec(memory_space=pltpu.SMEM)] + [VMEM] * 5,
        scratch=[
            pltpu.SMEM((items + 3 * batch,), jnp.int32),
            pltpu.VMEM((items, heads, d), F32),
            pltpu.VMEM((items, heads, d), F32),
        ],
        mib=12,
        name="suffix",
        flops=4 * rows * heads * slots * d,
        moved=4 * rows * slots * d,
    )
    operands = (*local, *returned)
    return call(
        partial(merge_kernel, kv_heads=kv_heads, group=group),
        jax.ShapeDtypeStruct((rows, heads, d), BF16),
        operands,
        [VMEM] * len(operands),
        mib=16,
        name="merge",
    )


def solution(mesh):
    placed = (
        P(("groups", "ctx"), "head", None),
        P(("groups", "ctx"), "head", None),
        P(("groups", "ctx"), "head", None),
        P(("groups", "ctx"), None, "head", None),
        P(("groups", "ctx"), None, "head", None),
        P(("groups", "ctx")),
    )
    return jax.shard_map(
        shards,
        mesh=mesh,
        in_specs=placed,
        out_specs=P(("groups", "ctx"), "head", None),
        check_vma=False,
    )
```

profile of v0, /device:TPU:0, one launch (start us, length us, event | category | flops | bytes accessed | tf_op | source)
XLA Modules:
  0.0 24.0 jit_solution(10428415649641865537)
XLA Ops:
  0.0 0.5 %collective-permute-start.2 = (bf16[4096,128]{1,0:T(8,128)(2,1)}, bf16[4096,128]{1,0:T(8,128)(2,1)S(1)}, u32[]{:S(2)}, u32[]{:S(2)}) collective-permute-start(bf16[4096,128]{1,0:T(8,128)(2,1)} %bitcast.37), channel_id=1, source_target_pairs={{0,4},{4,0},{8,12},{12,8},{1,5},{5,1},{9,13},{13,9},{2,6},{6,2},{1... | collective-permute-start | bytes 3145736 | tf_op jit(solution)/shard_map/ppermute | solution.py:274
  0.5 0.1 collective-permute-start.1
  0.5 2.9 %collective-permute-start = (bf16[48,16,128]{2,1,0:T(8,128)(2,1)}, bf16[48,16,128]{2,1,0:T(8,128)(2,1)S(1)}, u32[]{:S(2)}, u32[]{:S(2)}) collective-permute-start(bf16[48,16,128]{2,1,0:T(8,128)(2,1)} %q_ref.1), channel_id=1, source_target_pairs={{0,8},{4,12},{8,0},{12,4},{1,9},{5,13},{9,1},{13,5},{2,10},{6,14},... | collective-permute-start | bytes 589832 | tf_op jit(solution)/shard_map/ppermute | solution.py:230
  3.5 1.0 %copy_bitcast_fusion.4.q_ref = bf16[2,384,128]{2,1,0:T(8,128)(2,1)S(1)} fusion(bf16[48,16,128]{2,1,0:T(8,128)(2,1)} %q_ref.1), kind=kLoop, calls=%fused_computation.4 | loop fusion | bytes 393216 | tf_op jit(solution)/shard_map/reshape | solution.py:246
  4.5 0.0 collective-permute-done.2
  4.5 0.1 copy.18
  4.6 0.0 collective-permute-done.1
  4.6 0.1 copy.19
  4.8 2.1 %own.2 = (f32[2,384,128]{2,1,0:T(8,128)S(1)}, f32[2,384,128]{2,1,0:T(8,128)S(1)}) custom-call(bf16[2,384,128]{2,1,0:T(8,128)(2,1)S(1)} %copy_bitcast_fusion.4.q_ref, bf16[2,2048,128]{2,1,0:T(8,128)(2,1)S(1)} %bitcast.33, bf16[2,2048,128]{2,1,0:T(8,128)(2,1)S(1)} %bitcast.31), custom_call_target="tpu_custom_call" | custom-call | flops 3221225472 | bytes 2097152 | tf_op jit(solution)/shard_map/own/pallas_call | solution.py:234
  6.9 0.0 slice-start.3
  6.9 0.3 %copy_bitcast_fusion = (bf16[2,2048,128]{2,1,0:T(8,128)(2,1)S(1)}, bf16[2,2048,128]{2,1,0:T(8,128)(2,1)S(1)}) fusion(bf16[2048,2,128]{2,1,0:T(2,128)(2,1)S(1)} %copy-done.2, bf16[2048,2,128]{2,1,0:T(2,128)(2,1)S(1)} %copy-done.3), kind=kLoop, calls=%fused_computation | loop fusion | bytes 4194304 | tf_op jit(solution)/shard_map/transpose | solution.py:249
  7.2 0.0 slice-start.4
  7.2 2.3 %own.3 = (f32[2,384,128]{2,1,0:T(8,128)S(1)}, f32[2,384,128]{2,1,0:T(8,128)S(1)}) custom-call(bf16[2,384,128]{2,1,0:T(8,128)(2,1)S(1)} %copy_bitcast_fusion.4.q_ref, bf16[2,2048,128]{2,1,0:T(8,128)(2,1)S(1)} %get-tuple-element.32.refs_0_.refs_2_, bf16[2,2048,128]{2,1,0:T(8,128)(2,1)S(1)} %get-tuple-element.31.refs_1_.refs_3_, ...), custom_call_target="tpu_custom_call" | custom-call | flops 3221225472 | bytes 2097152 | tf_op jit(solution)/shard_map/own/pallas_call | solution.py:234
  9.6 0.0 slice-start
  9.6 0.0 copy-start
  9.6 0.0 copy-start.1
  9.6 0.0 collective-permute-done.q_ref
  9.6 0.0 slice-start.2
  9.6 0.0 slice-start.5
  9.6 4.2 %visiting.1 = bf16[800,128]{1,0:T(8,128)(2,1)S(1)} custom-call(bf16[48,16,128]{2,1,0:T(8,128)(2,1)S(1)} %collective-permute-done.q_ref, bf16[2,2048,128]{2,1,0:T(8,128)(2,1)S(1)} %bitcast.34, bf16[2,2048,128]{2,1,0:T(8,128)(2,1)S(1)} %bitcast.32, bf16[2,2048,128]{2,1,0:T(8,128)(2,1)S(1)} %get-tuple-element.32.refs_0_.refs_2_, ...), custom_call_target="tpu_custom_call" | custom-call | flops 6442450944 | bytes 4194304 | tf_op jit(solution)/shard_map/visiting/pallas_call | solution.py:234
  13.9 2.8 %collective-permute-start.3 = (bf16[800,128]{1,0:T(8,128)(2,1)S(1)}, bf16[800,128]{1,0:T(8,128)(2,1)S(1)}, u32[]{:S(2)}, u32[]{:S(2)}) collective-permute-start(bf16[800,128]{1,0:T(8,128)(2,1)S(1)} %visiting.1), channel_id=1, source_target_pairs={{0,8},{4,12},{8,0},{12,4},{1,9},{5,13},{9,1},{13,5},{2,10},{6,14},... | collective-permute-start | bytes 614408 | tf_op jit(solution)/shard_map/ppermute | solution.py:230
  16.7 6.3 %suffix.1 = (f32[48,16,128]{2,1,0:T(8,128)S(1)}, f32[48,16,128]{2,1,0:T(8,128)S(1)}) custom-call(s32[48]{0:T(128)S(1)} %copy-done.1, bf16[48,16,128]{2,1,0:T(8,128)(2,1)S(1)} %copy-done, bf16[48,1024,128]{2,1,0:T(8,128)(2,1)S(1)} %bitcast.27, bf16[48,1024,128]{2,1,0:T(8,128)(2,1)S(1)} %bitcast.30, f32[2,384,128]{2,1,0:T(8,128)S(1)} %get-tuple-element.26.op_ref, ...), custom_call_target="tpu_custom_call" | custom-call | flops 402653184 | bytes 25165824 | tf_op jit(solution)/shard_map/suffix/pallas_call | solution.py:234
  23.0 0.0 collective-permute-done.3.refs_0_
  23.1 0.9 %merge.1 = bf16[48,16,128]{2,1,0:T(8,128)(2,1)} custom-call(f32[48,16,128]{2,1,0:T(8,128)S(1)} %get-tuple-element.28.os_ref, f32[48,16,128]{2,1,0:T(8,128)S(1)} %get-tuple-element.29.ls_ref, bf16[800,128]{1,0:T(8,128)(2,1)S(1)} %collective-permute-done.3.refs_0_), custom_call_target="tpu_custom_call" | custom-call | tf_op jit(solution)/shard_map/merge/pallas_call | solution.py:234
  (15 shorter events, 0.0 us)
Async XLA Ops:
  0.0 6.9 %copy-start.2 = (bf16[2048,2,128]{2,1,0:T(2,128)(2,1)S(1)}, bf16[2048,2,128]{2,1,0:T(2,128)(2,1)}, u32[]{:S(2)}) copy-start(bf16[2048,2,128]{2,1,0:T(2,128)(2,1)} %param.8) | copy-start | bytes 3145732
  0.0 6.9 %copy-start.3 = (bf16[2048,2,128]{2,1,0:T(2,128)(2,1)S(1)}, bf16[2048,2,128]{2,1,0:T(2,128)(2,1)}, u32[]{:S(2)}) copy-start(bf16[2048,2,128]{2,1,0:T(2,128)(2,1)} %param.7) | copy-start | bytes 3145732
  0.0 4.5 %collective-permute-start.2 = (bf16[4096,128]{1,0:T(8,128)(2,1)}, bf16[4096,128]{1,0:T(8,128)(2,1)S(1)}, u32[]{:S(2)}, u32[]{:S(2)}) collective-permute-start(bf16[4096,128]{1,0:T(8,128)(2,1)} %bitcast.37), channel_id=1, source_target_pairs={{0,4},{4,0},{8,12},{12,8},{1,5},{5,1},{9,13},{13,9},{2,6},{6,2},{1... | collective-permute-start | bytes 3145736 | tf_op jit(solution)/shard_map/ppermute | solution.py:274
  0.5 4.2 %collective-permute-start.1 = (bf16[4096,128]{1,0:T(8,128)(2,1)}, bf16[4096,128]{1,0:T(8,128)(2,1)S(1)}, u32[]{:S(2)}, u32[]{:S(2)}) collective-permute-start(bf16[4096,128]{1,0:T(8,128)(2,1)} %bitcast.38), channel_id=1, source_target_pairs={{0,4},{4,0},{8,12},{12,8},{1,5},{5,1},{9,13},{13,9},{2,6},{6,2},{1... | collective-permute-start | bytes 3145736 | tf_op jit(solution)/shard_map/ppermute | solution.py:274
  0.5 9.1 %collective-permute-start = (bf16[48,16,128]{2,1,0:T(8,128)(2,1)}, bf16[48,16,128]{2,1,0:T(8,128)(2,1)S(1)}, u32[]{:S(2)}, u32[]{:S(2)}) collective-permute-start(bf16[48,16,128]{2,1,0:T(8,128)(2,1)} %q_ref.1), channel_id=1, source_target_pairs={{0,8},{4,12},{8,0},{12,4},{1,9},{5,13},{9,1},{13,5},{2,10},{6,14},... | collective-permute-start | bytes 589832 | tf_op jit(solution)/shard_map/ppermute | solution.py:230
  6.9 9.7 %slice-start.3 = ((s8[12582912]{0:T(1024)(128)(4,1)}), s8[4194304]{0:T(1024)(128)(4,1)S(1)}, s32[]{:S(2)}) async-start(s8[12582912]{0:T(1024)(128)(4,1)} %bitcast.28), calls=%async_computation.3 | async-start | bytes 8388608
  7.2 9.4 %slice-start.4 = ((s8[12582912]{0:T(1024)(128)(4,1)}), s8[4194304]{0:T(1024)(128)(4,1)S(1)}, s32[]{:S(2)}) async-start(s8[12582912]{0:T(1024)(128)(4,1)} %bitcast.28), calls=%async_computation.4 | async-start | bytes 8388608
  9.6 7.1 %slice-start = ((s8[12582912]{0:T(1024)(128)(4,1)}), s8[4194304]{0:T(1024)(128)(4,1)S(1)}, s32[]{:S(2)}) async-start(s8[12582912]{0:T(1024)(128)(4,1)} %bitcast.25), calls=%async_computation | async-start | bytes 8388608
  9.6 7.1 %copy-start = (bf16[48,16,128]{2,1,0:T(8,128)(2,1)S(1)}, bf16[48,16,128]{2,1,0:T(8,128)(2,1)}, u32[]{:S(2)}) copy-start(bf16[48,16,128]{2,1,0:T(8,128)(2,1)} %q_ref.1) | copy-start | bytes 589828
  9.6 7.1 %copy-start.1 = (s32[48]{0:T(128)S(1)}, s32[48]{0:T(128)}, u32[]{:S(2)}) copy-start(s32[48]{0:T(128)} %len_ref.1) | copy-start | bytes 580
  9.6 7.1 %slice-start.1 = ((s8[12582912]{0:T(1024)(128)(4,1)}), s8[4194304]{0:T(1024)(128)(4,1)S(1)}, s32[]{:S(2)}) async-start(s8[12582912]{0:T(1024)(128)(4,1)} %bitcast.25), calls=%async_computation.1 | async-start | bytes 8388608
  9.6 7.1 %slice-start.2 = ((s8[12582912]{0:T(1024)(128)(4,1)}), s8[4194304]{0:T(1024)(128)(4,1)S(1)}, s32[]{:S(2)}) async-start(s8[12582912]{0:T(1024)(128)(4,1)} %bitcast.25), calls=%async_computation.2 | async-start | bytes 8388608
  9.6 7.1 %slice-start.5 = ((s8[12582912]{0:T(1024)(128)(4,1)}), s8[4194304]{0:T(1024)(128)(4,1)S(1)}, s32[]{:S(2)}) async-start(s8[12582912]{0:T(1024)(128)(4,1)} %bitcast.28), calls=%async_computation.5 | async-start | bytes 8388608
  13.9 9.2 %collective-permute-start.3 = (bf16[800,128]{1,0:T(8,128)(2,1)S(1)}, bf16[800,128]{1,0:T(8,128)(2,1)S(1)}, u32[]{:S(2)}, u32[]{:S(2)}) collective-permute-start(bf16[800,128]{1,0:T(8,128)(2,1)S(1)} %visiting.1), channel_id=1, source_target_pairs={{0,8},{4,12},{8,0},{12,4},{1,9},{5,13},{9,1},{13,5},{2,10},{6,14},... | collective-permute-start | bytes 614408 | tf_op jit(solution)/shard_map/ppermute | solution.py:230
where the time goes:
time: 24.4 us; the launch traced here: 24 us
  Pallas kernels  16 us (66%)
  starting transfers between devices  6.21 us (25%)
  local copies, waits for them, and re-layouts  1.61 us (7%)
    pallas_call x5, Pallas kernels, call(): pl.pallas_call(kernel, out_shape=out_shape, in_specs=specs, out_specs=VME...  16 us
    ppermute x2, starting transfers between devices, shift(): return lax.ppermute(x, 'ctx', [(i, (i + by) % n) for i in range(n)])  5.68 us
    reshape x1, local copies, waits for them, and re-layouts, shards(): queries.reshape(rows, kv_heads, group, d).transpose(1, 0, 2, 3)  0.99 us
    ppermute x2, starting transfers between devices, shards(): flat = [by_head(lax.ppermute(x, 'ctx', swap)) for x in raw]  0.53 us
  transfers between devices with their start and end apart: 4, of which 0 were waited for; matrix products, arithmetic and copies ran while one was open for 6% of the time, Pallas kernels for 45%

commit v1 on v0

--- a/solution.py
+++ b/solution.py
@@ -103,8 +103,27 @@
         lse_ref[h] = jnp.broadcast_to(lse, o.shape)
 
 
+def queries_kernel(len_ref, q_hbm, o_ref, item_ref, q_ref, sem, *, kv_heads, chunk, chunks, pad):
+    copy = pltpu.make_async_copy(q_hbm, q_ref, sem)
+    copy.start()
+    rows = q_ref.shape[0]
+
+    def enlist(r, count):
+        for j in range(chunks):
+            item_ref[count + j] = r * chunks + j
+        return count + (len_ref[r] + chunk - 1) // chunk
+
+    count = lax.fori_loop(0, rows, enlist, 0, unroll=16 if rows % 16 == 0 else 1)
+    for j in range(pad):
+        item_ref[count + j] = 0
+    item_ref[rows * chunks + pad] = count
+    copy.wait()
+    for h, q in enumerate(split_heads(q_ref, kv_heads)):
+        o_ref[h] = q
+
+
 def suffix_kernel(
-    len_ref, q_ref, k_ref, v_ref, op_ref, lp_ref, o_ref, lse_ref, item_ref, oi_ref, li_ref, *, c, kv_heads, batch, chunk
+    len_ref, item_ref, q_ref, k_ref, v_ref, op_ref, lp_ref, o_ref, lse_ref, oi_ref, li_ref, *, c, kv_heads, batch, chunk
 ):
     rows, heads, d = q_ref.shape
     group = heads // kv_heads
@@ -114,14 +133,7 @@
     head = lax.broadcasted_iota(jnp.int32, (heads, width), 0) // group
     place = jnp.where(lane % kv_heads == head, lane // kv_heads, chunk * chunks)
 
-    def enlist(r, count):
-        for j in range(chunks):
-            item_ref[count + j] = r * chunks + j
-        return count + (len_ref[r] + chunk - 1) // chunk
-
-    count = lax.fori_loop(0, rows, enlist, 0)
-    for j in range(2 * batch):
-        item_ref[count + j] = 0
+    count = item_ref[rows * chunks + 2 * batch]
     batches = (count + batch - 1) // batch
 
     def part(slot):
@@ -229,13 +241,13 @@
     def shift(x, by):
         return lax.ppermute(x, "ctx", [(i, (i + by) % n) for i in range(n)])
 
-    def call(kernel, out_shape, operands, specs, scratch=(), mib=40, name=None, flops=0, moved=0):
+    def call(kernel, out_shape, operands, specs, scratch=(), outs=None, mib=40, name=None, flops=0, moved=0):
         single = not isinstance(out_shape, tuple)
         return pl.pallas_call(
             kernel,
             out_shape=out_shape,
             in_specs=specs,
-            out_specs=VMEM if single else (VMEM,) * len(out_shape),
+            out_specs=outs or (VMEM if single else (VMEM,) * len(out_shape)),
             scratch_shapes=scratch,
             compiler_params=pltpu.CompilerParams(vmem_limit_bytes=mib << 20),
             cost_estimate=pl.CostEstimate(flops=flops, bytes_accessed=moved, transcendentals=0),
@@ -243,7 +255,22 @@
         )(*operands)
 
     raw = [prefix_keys.reshape(-1, d), prefix_values.reshape(-1, d)]
-    split_queries = queries.reshape(rows, kv_heads, group, d).transpose(1, 0, 2, 3).reshape(kv_heads, m, d)
+    slots = span * kv_heads
+    chunk = 128 if span % 128 == 0 else span
+    batch = 16
+    items = rows * (span // chunk)
+    smem = pl.BlockSpec(memory_space=pltpu.SMEM)
+    split_queries, table = call(
+        partial(queries_kernel, kv_heads=kv_heads, chunk=chunk, chunks=span // chunk, pad=2 * batch),
+        (jax.ShapeDtypeStruct((kv_heads, m, d), BF16), jax.ShapeDtypeStruct((items + 2 * batch + 1,), jnp.int32)),
+        (lengths, pltpu.with_memory_space_constraint(queries, pltpu.HBM)),
+        [smem, pl.BlockSpec(memory_space=pltpu.HBM)],
+        scratch=[pltpu.VMEM((rows, heads, d), BF16), pltpu.SemaphoreType.DMA],
+        outs=(VMEM, smem),
+        mib=16,
+        name="queries",
+        moved=4 * m * kv_heads * d,
+    )
 
     def by_head(x):
         return x.reshape(-1, kv_heads, d).transpose(1, 0, 2)
@@ -292,17 +319,12 @@
             moved=cores * moved,
         )
         returned.append(shift(msg, -(j + 1) * cores))
-    slots = span * kv_heads
-    chunk = 128 if span % 128 == 0 else span
-    batch = 16
-    items = rows * (span // chunk)
     local = call(
         partial(suffix_kernel, c=c, kv_heads=kv_heads, batch=batch, chunk=chunk),
         (jax.ShapeDtypeStruct((rows, heads, d), F32),) * 2,
-        (lengths, queries, suffix_keys.reshape(rows, slots, d), suffix_values.reshape(rows, slots, d), own_o, own_l),
-        [pl.BlockSpec(memory_space=pltpu.SMEM)] + [VMEM] * 5,
+        (lengths, table, queries, suffix_keys.reshape(rows, slots, d), suffix_values.reshape(rows, slots, d), own_o, own_l),
+        [smem] * 2 + [VMEM] * 5,
         scratch=[
-            pltpu.SMEM((items + 3 * batch,), jnp.int32),
             pltpu.VMEM((items, heads, d), F32),
             pltpu.VMEM((items, heads, d), F32),
         ],

time: 24.4 us -> 25.5 us (1.045); the launches traced: 24 us -> 25.4 us
  Pallas kernels: 16 us -> 18.8 us
  starting transfers between devices: 6.21 us -> 4.37 us
  local copies, waits for them, and re-layouts: 1.61 us -> 1.97 us
    pallas_call x5 -> x6, Pallas kernels: 16 us -> 18.8 us  [call(): pl.pallas_call(kernel, out_shape=out_shape, in_specs=specs, out_specs=out...]
    ppermute x2, starting transfers between devices: 5.68 us -> 3.86 us  [shift(): return lax.ppermute(x, 'ctx', [(i, (i + by) % n) for i in range(n)])]
    unnamed x20 -> x22, local copies, waits for them, and re-layouts: 0.06 us -> 1.41 us
    reshape x1 -> x0, local copies, waits for them, and re-layouts: 0.99 us -> none  [shards(): queries.reshape(rows, kv_heads, group, d).transpose(1, 0, 2, 3)]
  transfers between devices with their start and end apart: 4 -> 4, of which waited for: 0 -> 0; matrix products, arithmetic and copies ran while one was open for 6% -> 2% of each run, Pallas kernels for 45% -> 54%
where the time goes in v1:
time: 25.5 us; the launch traced here: 25.4 us
  Pallas kernels  18.8 us (74%)
  starting transfers between devices  4.37 us (17%)
  local copies, waits for them, and re-layouts  1.97 us (8%)
    pallas_call x6, Pallas kernels, call(): pl.pallas_call(kernel, out_shape=out_shape, in_specs=specs, out_specs=out...  18.8 us
    ppermute x2, starting transfers between devices, shift(): return lax.ppermute(x, 'ctx', [(i, (i + by) % n) for i in range(n)])  3.86 us
    unnamed x22, local copies, waits for them, and re-layouts  1.41 us
    ppermute x2, starting transfers between devices, shards(): flat = [by_head(lax.ppermute(x, 'ctx', swap)) for x in raw]  0.51 us
  transfers between devices with their start and end apart: 4, of which 0 were waited for; matrix products, arithmetic and copies ran while one was open for 2% of the time, Pallas kernels for 54%

profile of v1, /device:TPU:0, one launch (start us, length us, event | category | flops | bytes accessed | tf_op | source)
XLA Modules:
  0.0 25.4 jit_solution(7230251084236608852)
XLA Ops:
  0.0 0.5 %collective-permute-start.2 = (bf16[4096,128]{1,0:T(8,128)(2,1)}, bf16[4096,128]{1,0:T(8,128)(2,1)S(1)}, u32[]{:S(2)}, u32[]{:S(2)}) collective-permute-start(bf16[4096,128]{1,0:T(8,128)(2,1)} %bitcast.30), channel_id=1, source_target_pairs={{0,4},{4,0},{8,12},{12,8},{1,5},{5,1},{9,13},{13,9},{2,6},{6,2},{1... | collective-permute-start | bytes 3145736 | tf_op jit(solution)/shard_map/ppermute | solution.py:301
  0.5 0.1 collective-permute-start.1
  0.5 2.9 %collective-permute-start = (bf16[48,16,128]{2,1,0:T(8,128)(2,1)}, bf16[48,16,128]{2,1,0:T(8,128)(2,1)S(1)}, u32[]{:S(2)}, u32[]{:S(2)}) collective-permute-start(bf16[48,16,128]{2,1,0:T(8,128)(2,1)} %q_ref.1), channel_id=1, source_target_pairs={{0,8},{4,12},{8,0},{12,4},{1,9},{5,13},{9,1},{13,5},{2,10},{6,14},... | collective-permute-start | bytes 589832 | tf_op jit(solution)/shard_map/ppermute | solution.py:242
  3.5 0.7 %copy-done.1 = s32[48]{0:T(128)S(1)} copy-done((s32[48]{0:T(128)S(1)}, s32[48]{0:T(128)}, u32[]{:S(2)}) %copy-start.1) | copy-done | bytes 216
  4.1 2.2 %queries.1 = (bf16[2,384,128]{2,1,0:T(8,128)(2,1)S(1)}, s32[225]{0:T(256)S(1)}) custom-call(s32[48]{0:T(128)S(1)} %copy-done.1, bf16[48,16,128]{2,1,0:T(8,128)(2,1)} %q_ref.1), custom_call_target="tpu_custom_call" | custom-call | bytes 393216 | tf_op jit(solution)/shard_map/queries/pallas_call | solution.py:246
  6.3 0.1 copy.15
  6.4 0.0 collective-permute-done.1
  6.4 0.1 copy.16
  6.6 2.1 %own.2 = (f32[2,384,128]{2,1,0:T(8,128)S(1)}, f32[2,384,128]{2,1,0:T(8,128)S(1)}) custom-call(bf16[2,384,128]{2,1,0:T(8,128)(2,1)S(1)} %get-tuple-element.21.q_ref, bf16[2,2048,128]{2,1,0:T(8,128)(2,1)S(1)} %bitcast.26, bf16[2,2048,128]{2,1,0:T(8,128)(2,1)S(1)} %bitcast.24), custom_call_target="tpu_custom_call" | custom-call | flops 3221225472 | bytes 2097152 | tf_op jit(solution)/shard_map/own/pallas_call | solution.py:246
  8.7 0.0 slice-start.3
  8.8 0.3 %copy_bitcast_fusion = (bf16[2,2048,128]{2,1,0:T(8,128)(2,1)S(1)}, bf16[2,2048,128]{2,1,0:T(8,128)(2,1)S(1)}) fusion(bf16[2048,2,128]{2,1,0:T(2,128)(2,1)S(1)} %copy-done.3, bf16[2048,2,128]{2,1,0:T(2,128)(2,1)S(1)} %copy-done.4), kind=kLoop, calls=%fused_computation | loop fusion | bytes 4194304 | tf_op jit(solution)/shard_map/transpose | solution.py:276
  9.0 0.0 slice-start.4
  9.0 2.3 %own.3 = (f32[2,384,128]{2,1,0:T(8,128)S(1)}, f32[2,384,128]{2,1,0:T(8,128)S(1)}) custom-call(bf16[2,384,128]{2,1,0:T(8,128)(2,1)S(1)} %get-tuple-element.21.q_ref, bf16[2,2048,128]{2,1,0:T(8,128)(2,1)S(1)} %get-tuple-element.36.refs_0_.refs_2_, bf16[2,2048,128]{2,1,0:T(8,128)(2,1)S(1)} %get-tuple-element.35.refs_1_.refs_3_, ...), custom_call_target="tpu_custom_call" | custom-call | flops 3221225472 | bytes 2097152 | tf_op jit(solution)/shard_map/own/pallas_call | solution.py:246
  11.4 0.0 slice-start
  11.4 0.0 copy-start
  11.4 0.0 copy-start.2
  11.5 0.0 slice-start.2
  11.5 0.0 slice-start.5
  11.5 4.3 %visiting.1 = bf16[800,128]{1,0:T(8,128)(2,1)S(1)} custom-call(bf16[48,16,128]{2,1,0:T(8,128)(2,1)S(1)} %collective-permute-done.q_ref, bf16[2,2048,128]{2,1,0:T(8,128)(2,1)S(1)} %bitcast.27, bf16[2,2048,128]{2,1,0:T(8,128)(2,1)S(1)} %bitcast.25, bf16[2,2048,128]{2,1,0:T(8,128)(2,1)S(1)} %get-tuple-element.36.refs_0_.refs_2_, ...), custom_call_target="tpu_custom_call" | custom-call | flops 6442450944 | bytes 4194304 | tf_op jit(solution)/shard_map/visiting/pallas_call | solution.py:246
  15.8 0.9 %collective-permute-start.3 = (bf16[800,128]{1,0:T(8,128)(2,1)S(1)}, bf16[800,128]{1,0:T(8,128)(2,1)S(1)}, u32[]{:S(2)}, u32[]{:S(2)}) collective-permute-start(bf16[800,128]{1,0:T(8,128)(2,1)S(1)} %visiting.1), channel_id=1, source_target_pairs={{0,8},{4,12},{8,0},{12,4},{1,9},{5,13},{9,1},{13,5},{2,10},{6,14},... | collective-permute-start | bytes 614408 | tf_op jit(solution)/shard_map/ppermute | solution.py:242
  16.7 0.7 %slice-done.5 = s8[4194304]{0:T(1024)(128)(4,1)S(1)} async-done(((s8[12582912]{0:T(1024)(128)(4,1)}), s8[4194304]{0:T(1024)(128)(4,1)S(1)}, s32[]{:S(2)}) %slice-start.5) | async-done | bytes 4194328
  17.4 7.0 %suffix.1 = (f32[48,16,128]{2,1,0:T(8,128)S(1)}, f32[48,16,128]{2,1,0:T(8,128)S(1)}) custom-call(s32[48]{0:T(128)S(1)} %copy-done.2, s32[225]{0:T(256)S(1)} %get-tuple-element.20.item_ref, bf16[48,16,128]{2,1,0:T(8,128)(2,1)S(1)} %copy-done, bf16[48,1024,128]{2,1,0:T(8,128)(2,1)S(1)} %bitcast.20, bf16[48,1024,128]{2,1,0:T(8,128)(2,1)S(1)} %bitcast.23, ...), custom_call_target="tpu_custom_call" | custom-call | flops 402653184 | bytes 25165824 | tf_op jit(solution)/shard_map/suffix/pallas_call | solution.py:246
  24.4 0.0 collective-permute-done.3.refs_0_
  24.4 0.9 %merge.1 = bf16[48,16,128]{2,1,0:T(8,128)(2,1)} custom-call(f32[48,16,128]{2,1,0:T(8,128)S(1)} %get-tuple-element.32.os_ref, f32[48,16,128]{2,1,0:T(8,128)S(1)} %get-tuple-element.33.ls_ref, bf16[800,128]{1,0:T(8,128)(2,1)S(1)} %collective-permute-done.3.refs_0_), custom_call_target="tpu_custom_call" | custom-call | tf_op jit(solution)/shard_map/merge/pallas_call | solution.py:246
  (17 shorter events, 0.0 us)
Async XLA Ops:
  0.0 6.3 %collective-permute-start.2 = (bf16[4096,128]{1,0:T(8,128)(2,1)}, bf16[4096,128]{1,0:T(8,128)(2,1)S(1)}, u32[]{:S(2)}, u32[]{:S(2)}) collective-permute-start(bf16[4096,128]{1,0:T(8,128)(2,1)} %bitcast.30), channel_id=1, source_target_pairs={{0,4},{4,0},{8,12},{12,8},{1,5},{5,1},{9,13},{13,9},{2,6},{6,2},{1... | collective-permute-start | bytes 3145736 | tf_op jit(solution)/shard_map/ppermute | solution.py:301
  0.5 6.0 %collective-permute-start.1 = (bf16[4096,128]{1,0:T(8,128)(2,1)}, bf16[4096,128]{1,0:T(8,128)(2,1)S(1)}, u32[]{:S(2)}, u32[]{:S(2)}) collective-permute-start(bf16[4096,128]{1,0:T(8,128)(2,1)} %bitcast.31), channel_id=1, source_target_pairs={{0,4},{4,0},{8,12},{12,8},{1,5},{5,1},{9,13},{13,9},{2,6},{6,2},{1... | collective-permute-start | bytes 3145736 | tf_op jit(solution)/shard_map/ppermute | solution.py:301
  0.5 10.9 %collective-permute-start = (bf16[48,16,128]{2,1,0:T(8,128)(2,1)}, bf16[48,16,128]{2,1,0:T(8,128)(2,1)S(1)}, u32[]{:S(2)}, u32[]{:S(2)}) collective-permute-start(bf16[48,16,128]{2,1,0:T(8,128)(2,1)} %q_ref.1), channel_id=1, source_target_pairs={{0,8},{4,12},{8,0},{12,4},{1,9},{5,13},{9,1},{13,5},{2,10},{6,14},... | collective-permute-start | bytes 589832 | tf_op jit(solution)/shard_map/ppermute | solution.py:242
  3.5 0.7 %copy-start.1 = (s32[48]{0:T(128)S(1)}, s32[48]{0:T(128)}, u32[]{:S(2)}) copy-start(s32[48]{0:T(128)} %len_ref.3) | copy-start | bytes 580
  4.1 4.6 %copy-start.3 = (bf16[2048,2,128]{2,1,0:T(2,128)(2,1)S(1)}, bf16[2048,2,128]{2,1,0:T(2,128)(2,1)}, u32[]{:S(2)}) copy-start(bf16[2048,2,128]{2,1,0:T(2,128)(2,1)} %param.8) | copy-start | bytes 3145732
  4.1 4.6 %copy-start.4 = (bf16[2048,2,128]{2,1,0:T(2,128)(2,1)S(1)}, bf16[2048,2,128]{2,1,0:T(2,128)(2,1)}, u32[]{:S(2)}) copy-start(bf16[2048,2,128]{2,1,0:T(2,128)(2,1)} %param.7) | copy-start | bytes 3145732
  8.7 8.0 %slice-start.3 = ((s8[12582912]{0:T(1024)(128)(4,1)}), s8[4194304]{0:T(1024)(128)(4,1)S(1)}, s32[]{:S(2)}) async-start(s8[12582912]{0:T(1024)(128)(4,1)} %bitcast.21), calls=%async_computation.3 | async-start | bytes 8388608
  9.0 7.7 %slice-start.4 = ((s8[12582912]{0:T(1024)(128)(4,1)}), s8[4194304]{0:T(1024)(128)(4,1)S(1)}, s32[]{:S(2)}) async-start(s8[12582912]{0:T(1024)(128)(4,1)} %bitcast.21), calls=%async_computation.4 | async-start | bytes 8388608
  11.4 5.3 %slice-start = ((s8[12582912]{0:T(1024)(128)(4,1)}), s8[4194304]{0:T(1024)(128)(4,1)S(1)}, s32[]{:S(2)}) async-start(s8[12582912]{0:T(1024)(128)(4,1)} %bitcast.18), calls=%async_computation | async-start | bytes 8388608
  11.4 5.3 %copy-start = (bf16[48,16,128]{2,1,0:T(8,128)(2,1)S(1)}, bf16[48,16,128]{2,1,0:T(8,128)(2,1)}, u32[]{:S(2)}) copy-start(bf16[48,16,128]{2,1,0:T(8,128)(2,1)} %q_ref.1) | copy-start | bytes 589828
  11.4 5.3 %copy-start.2 = (s32[48]{0:T(128)S(1)}, s32[48]{0:T(128)}, u32[]{:S(2)}) copy-start(s32[48]{0:T(128)} %len_ref.3) | copy-start | bytes 580
  11.4 5.3 %slice-start.1 = ((s8[12582912]{0:T(1024)(128)(4,1)}), s8[4194304]{0:T(1024)(128)(4,1)S(1)}, s32[]{:S(2)}) async-start(s8[12582912]{0:T(1024)(128)(4,1)} %bitcast.18), calls=%async_computation.1 | async-start | bytes 8388608
  11.5 5.3 %slice-start.2 = ((s8[12582912]{0:T(1024)(128)(4,1)}), s8[4194304]{0:T(1024)(128)(4,1)S(1)}, s32[]{:S(2)}) async-start(s8[12582912]{0:T(1024)(128)(4,1)} %bitcast.18), calls=%async_computation.2 | async-start | bytes 8388608
  11.5 6.0 %slice-start.5 = ((s8[12582912]{0:T(1024)(128)(4,1)}), s8[4194304]{0:T(1024)(128)(4,1)S(1)}, s32[]{:S(2)}) async-start(s8[12582912]{0:T(1024)(128)(4,1)} %bitcast.21), calls=%async_computation.5 | async-start | bytes 8388608
  15.8 8.7 %collective-permute-start.3 = (bf16[800,128]{1,0:T(8,128)(2,1)S(1)}, bf16[800,128]{1,0:T(8,128)(2,1)S(1)}, u32[]{:S(2)}, u32[]{:S(2)}) collective-permute-start(bf16[800,128]{1,0:T(8,128)(2,1)S(1)} %visiting.1), channel_id=1, source_target_pairs={{0,8},{4,12},{8,0},{12,4},{1,9},{5,13},{9,1},{13,5},{2,10},{6,14},... | collective-permute-start | bytes 614408 | tf_op jit(solution)/shard_map/ppermute | solution.py:242

commit v2 on v1

--- a/solution.py
+++ b/solution.py
@@ -27,12 +27,22 @@
     return lax.dot_general(q, k, (((1,), (1,)), ((), ())), preferred_element_type=F32)
 
 
-def attend_blocks(heads_q, kv_refs, c):
+def attend_blocks(heads_q, kv_refs, c, ready=()):
     d = heads_q[0].shape[1]
     blocks = len(kv_refs) // 2
     items = [(h, b) for h in range(len(heads_q)) for b in range(blocks)]
     parts = {}
+    ready = list(ready)
     s = w = None
+
+    def weigh(w, top, v):
+        oa = jnp.dot(w, jnp.concatenate([v, jnp.ones_like(v)], axis=1), preferred_element_type=F32)
+        return oa[:, :d], oa[:, d:], top
+
+    def take_ready():
+        h, *rest = ready.pop(0)
+        parts[h, blocks] = weigh(*rest)
+
     for step in range(len(items) + 2):
         s_next = w_next = None
         if step < len(items):
@@ -40,22 +50,24 @@
             s_next = scores_of(heads_q[h], kv_refs[2 * b][h])
         if w is not None:
             h, b = items[step - 2]
-            v = kv_refs[2 * b + 1][h]
-            oa = jnp.dot(w[0], jnp.concatenate([v, jnp.ones_like(v)], axis=1), preferred_element_type=F32)
-            parts[h, b] = (oa[:, :d], oa[:, d:], w[1])
+            parts[h, b] = weigh(*w, kv_refs[2 * b + 1][h])
+        elif ready:
+            take_ready()
         if s is not None:
             top = jnp.max(s, axis=1, keepdims=True)
             w_next = (jnp.exp2(s * c - top * c).astype(BF16), top * c)
         s, w = s_next, w_next
+    while ready:
+        take_ready()
     results = []
     for h in range(len(heads_q)):
-        top = parts[h, 0][2]
-        for b in range(1, blocks):
-            top = jnp.maximum(top, parts[h, b][2])
+        mine = [parts[h, b] for b in range(blocks + 1) if (h, b) in parts]
+        top = mine[0][2]
+        for part in mine[1:]:
+            top = jnp.maximum(top, part[2])
         acc = 0.0
         total = 0.0
-        for b in range(blocks):
-            o, l, t = parts[h, b]
+        for o, l, t in mine:
             scale = jnp.exp2(t - top)
             acc = acc + o * scale
             total = total + l * scale
@@ -88,24 +100,32 @@
     msg_ref[kv_heads * m :, :] = jnp.concatenate(out, axis=0).astype(BF16)
 
 
-def own_kernel(q_ref, *refs, c, kv_heads, blocks):
-    kv_refs, before, (o_ref, lse_ref) = refs[: 2 * blocks], refs[2 * blocks : -2], refs[-2:]
+def first_kernel(q_ref, k_ref, w_ref, top_ref, *, c, kv_heads):
+    scores = [scores_of(q_ref[h], k_ref[h]) for h in range(kv_heads)]
+    for h in range(kv_heads):
+        top = jnp.max(scores[h], axis=1, keepdims=True)
+        w_ref[h] = jnp.exp2(scores[h] * c - top * c).astype(BF16)
+        top_ref[h] = jnp.broadcast_to(top * c, top_ref.shape[1:])
+
+
+def own_kernel(q_ref, k_ref, v_ref, *refs, c, kv_heads):
+    before, (o_ref, lse_ref) = refs[:-2], refs[-2:]
     heads_q = [q_ref[h] for h in range(kv_heads)]
-    for h, (o, lse) in enumerate(attend_blocks(heads_q, kv_refs, c)):
-        if before:
-            o_old, lse_old = before[0][h], before[1][h]
-            top = jnp.maximum(lse, lse_old)
-            new, old = jnp.exp2(lse - top), jnp.exp2(lse_old - top)
-            total = new + old
-            o = (o * new + o_old * old) / total
-            lse = top + jnp.log2(total)
+    ready = ()
+    if before:
+        w_ref, top_ref, late_ref = before
+        ready = [(h, w_ref[h], top_ref[h][:, :1], late_ref[h]) for h in range(kv_heads)]
+    for h, (o, lse) in enumerate(attend_blocks(heads_q, (k_ref, v_ref), c, ready)):
         o_ref[h] = o
         lse_ref[h] = jnp.broadcast_to(lse, o.shape)
 
 
-def queries_kernel(len_ref, q_hbm, o_ref, item_ref, q_ref, sem, *, kv_heads, chunk, chunks, pad):
-    copy = pltpu.make_async_copy(q_hbm, q_ref, sem)
+def queries_kernel(len_hbm, q_hbm, o_ref, item_ref, len_ref, q_ref, sems, *, kv_heads, chunk, chunks, pad):
+    numbers = pltpu.make_async_copy(len_hbm, len_ref, sems.at[0])
+    numbers.start()
+    copy = pltpu.make_async_copy(q_hbm, q_ref, sems.at[1])
     copy.start()
+    numbers.wait()
     rows = q_ref.shape[0]
 
     def enlist(r, count):
@@ -263,9 +283,9 @@
     split_queries, table = call(
         partial(queries_kernel, kv_heads=kv_heads, chunk=chunk, chunks=span // chunk, pad=2 * batch),
         (jax.ShapeDtypeStruct((kv_heads, m, d), BF16), jax.ShapeDtypeStruct((items + 2 * batch + 1,), jnp.int32)),
-        (lengths, pltpu.with_memory_space_constraint(queries, pltpu.HBM)),
-        [smem, pl.BlockSpec(memory_space=pltpu.HBM)],
-        scratch=[pltpu.VMEM((rows, heads, d), BF16), pltpu.SemaphoreType.DMA],
+        [pltpu.with_memory_space_constraint(x, pltpu.HBM) for x in (lengths, queries)],
+        [pl.BlockSpec(memory_space=pltpu.HBM)] * 2,
+        scratch=[pltpu.SMEM((rows,), jnp.int32), pltpu.VMEM((rows, heads, d), BF16), pltpu.SemaphoreType.DMA((2,))],
         outs=(VMEM, smem),
         mib=16,
         name="queries",
@@ -278,31 +298,40 @@
     visiting = [shift(queries, j * cores) for j in range(1, chips)]
 
     spread = prefix_keys.shape[0]
-    flops = 16 * m * kv_heads * spread * d
+    flops = 12 * m * kv_heads * spread * d
     moved = 4 * kv_heads * spread * d
 
-    def own_rows(kv, before):
-        operands = (split_queries, *kv, *before)
-        return call(
-            partial(own_kernel, c=c, kv_heads=kv_heads, blocks=len(kv) // 2),
-            (jax.ShapeDtypeStruct((kv_heads, m, d), F32),) * 2,
-            operands,
-            [VMEM] * len(operands),
+    flat = []
+    before = ()
+    if cores == 2:
+        swap = [(i, i ^ 1) for i in range(n)]
+        keys, values = [lax.ppermute(x, "ctx", swap) for x in raw]
+        keys = by_head(keys)
+        weights = call(
+            partial(first_kernel, c=c, kv_heads=kv_heads),
+            (jax.ShapeDtypeStruct((kv_heads, m, spread), BF16), jax.ShapeDtypeStruct((kv_heads, m, d), F32)),
+            (split_queries, keys),
+            [VMEM] * 2,
             mib=24,
-            name="own",
-            flops=flops,
+            name="first",
+            flops=3 * flops // 2,
             moved=moved,
         )
-
-    flat = []
-    own = ()
-    if cores == 2:
-        swap = [(i, i ^ 1) for i in range(n)]
-        flat = [by_head(lax.ppermute(x, "ctx", swap)) for x in raw]
-        own = own_rows(flat, ())
-        raw, own = lax.optimization_barrier((raw, own))
+        raw, values, weights = lax.optimization_barrier((raw, values, weights))
+        flat = [keys, by_head(values)]
+        before = (*weights, flat[1])
     raw = [by_head(x) for x in raw]
-    own_o, own_l = own_rows(raw, own)
+    operands = (split_queries, *raw, *before)
+    own_o, own_l = call(
+        partial(own_kernel, c=c, kv_heads=kv_heads),
+        (jax.ShapeDtypeStruct((kv_heads, m, d), F32),) * 2,
+        operands,
+        [VMEM] * len(operands),
+        mib=24,
+        name="own",
+        flops=flops,
+        moved=moved,
+    )
     flat = [*flat, *raw]
     visiting, own_o, own_l = lax.optimization_barrier((visiting, own_o, own_l))
     message = jax.ShapeDtypeStruct((kv_heads * m + pieces, d), BF16)

time: 25.5 us -> 23 us (0.902)
  Pallas kernels: 18.8 us -> 16.8 us
  local copies, waits for them, and re-layouts: 1.97 us -> 0.61 us
  waiting for transfers between devices: 0.01 us -> 1.08 us
    pallas_call x6, Pallas kernels: 18.8 us -> 16.8 us  [call(): pl.pallas_call(kernel, out_shape=out_shape, in_specs=specs, out_specs=out...]
    unnamed x22 -> x20, local copies, waits for them, and re-layouts: 1.41 us -> 0.06 us
    ppermute x2, waiting for transfers between devices: 0.01 us -> 1.07 us  [shift(): return lax.ppermute(x, 'ctx', [(i, (i + by) % n) for i in range(n)])]
  transfers between devices with their start and end apart: 4 -> 4, of which waited for: 0 -> 1; matrix products, arithmetic and copies ran while one was open for 2% -> 2% of each run, Pallas kernels for 54% -> 51%
where the time goes in v2:
time: 23 us; the launch traced here: 22.8 us
  Pallas kernels  16.8 us (73%)
  starting transfers between devices  4.14 us (18%)
  waiting for transfers between devices  1.08 us (5%)
  local copies, waits for them, and re-layouts  0.61 us (3%)
    pallas_call x6, Pallas kernels, call(): pl.pallas_call(kernel, out_shape=out_shape, in_specs=specs, out_specs=out...  16.8 us
    ppermute x2, starting transfers between devices, shift(): return lax.ppermute(x, 'ctx', [(i, (i + by) % n) for i in range(n)])  3.61 us
    ppermute x2, waiting for transfers between devices, shift(): return lax.ppermute(x, 'ctx', [(i, (i + by) % n) for i in range(n)])  1.07 us
    ppermute x2, starting transfers between devices, shards(): keys, values = [lax.ppermute(x, 'ctx', swap) for x in raw]  0.53 us
  transfers between devices with their start and end apart: 4, of which 1 were waited for; matrix products, arithmetic and copies ran while one was open for 2% of the time, Pallas kernels for 51%

profile of v2, /device:TPU:0, one launch (start us, length us, event | category | flops | bytes accessed | tf_op | source)
XLA Modules:
  0.0 22.8 jit_solution(12934830841813320040)
XLA Ops:
  0.0 0.5 %collective-permute-start.2 = (bf16[4096,128]{1,0:T(8,128)(2,1)}, bf16[4096,128]{1,0:T(8,128)(2,1)S(1)}, u32[]{:S(2)}, u32[]{:S(2)}) collective-permute-start(bf16[4096,128]{1,0:T(8,128)(2,1)} %bitcast.28), channel_id=1, source_target_pairs={{0,4},{4,0},{8,12},{12,8},{1,5},{5,1},{9,13},{13,9},{2,6},{6,2},{1... | collective-permute-start | bytes 3145736 | tf_op jit(solution)/shard_map/ppermute | solution.py:308
  0.5 0.1 collective-permute-start.1
  0.5 2.9 %collective-permute-start = (bf16[48,16,128]{2,1,0:T(8,128)(2,1)}, bf16[48,16,128]{2,1,0:T(8,128)(2,1)S(1)}, u32[]{:S(2)}, u32[]{:S(2)}) collective-permute-start(bf16[48,16,128]{2,1,0:T(8,128)(2,1)} %q_ref.1), channel_id=1, source_target_pairs={{0,8},{4,12},{8,0},{12,4},{1,9},{5,13},{9,1},{13,5},{2,10},{6,14},... | collective-permute-start | bytes 589832 | tf_op jit(solution)/shard_map/ppermute | solution.py:262
  3.5 1.7 %queries.1 = (bf16[2,384,128]{2,1,0:T(8,128)(2,1)S(1)}, s32[225]{0:T(256)S(1)}) custom-call(s32[48]{0:T(128)} %len_ref.1, bf16[48,16,128]{2,1,0:T(8,128)(2,1)} %q_ref.1), custom_call_target="tpu_custom_call" | custom-call | bytes 393216 | tf_op jit(solution)/shard_map/queries/pallas_call | solution.py:266
  5.2 0.0 collective-permute-done.2
  5.2 0.1 copy.16
  5.3 0.0 slice-start.3
  5.3 1.9 %first.1 = (bf16[2,384,2048]{2,1,0:T(8,128)(2,1)S(1)}, f32[2,384,128]{2,1,0:T(8,128)S(1)}) custom-call(bf16[2,384,128]{2,1,0:T(8,128)(2,1)S(1)} %get-tuple-element.22.q_ref, bf16[2,2048,128]{2,1,0:T(8,128)(2,1)S(1)} %bitcast.24), custom_call_target="tpu_custom_call" | custom-call | flops 3623878656 | bytes 2097152 | tf_op jit(solution)/shard_map/first/pallas_call | solution.py:266
  7.2 0.0 collective-permute-done.1
  7.3 0.1 copy.15
  7.4 0.0 slice-start.4
  7.4 0.3 %copy_bitcast_fusion = (bf16[2,2048,128]{2,1,0:T(8,128)(2,1)S(1)}, bf16[2,2048,128]{2,1,0:T(8,128)(2,1)S(1)}) fusion(bf16[2048,2,128]{2,1,0:T(2,128)(2,1)S(1)} %bitcast.31, bf16[2048,2,128]{2,1,0:T(2,128)(2,1)S(1)} %copy-done.3), kind=kLoop, calls=%fused_computation | loop fusion | bytes 4194304 | tf_op jit(solution)/shard_map/transpose | solution.py:296
  7.7 0.0 slice-start
  7.7 0.0 copy-start
  7.7 0.0 copy-start.1
  7.8 3.1 %own.1 = (f32[2,384,128]{2,1,0:T(8,128)S(1)}, f32[2,384,128]{2,1,0:T(8,128)S(1)}) custom-call(bf16[2,384,128]{2,1,0:T(8,128)(2,1)S(1)} %get-tuple-element.22.q_ref, bf16[2,2048,128]{2,1,0:T(8,128)(2,1)S(1)} %bitcast.26, bf16[2,2048,128]{2,1,0:T(8,128)(2,1)S(1)} %get-tuple-element.38.v_ref.refs_3_, bf16[2,384,2048]{2,1,0:T(8,128)(2,1)S(1)} %get-tuple-element.27.refs_0_, ...), custom_call_target="tpu_custom_call" | custom-call | flops 2415919104 | bytes 2097152 | tf_op jit(solution)/shard_map/own/pallas_call | solution.py:266
  10.8 0.0 collective-permute-done.q_ref
  10.8 0.0 slice-start.1
  10.8 0.0 slice-start.5
  10.9 4.2 %visiting.1 = bf16[800,128]{1,0:T(8,128)(2,1)S(1)} custom-call(bf16[48,16,128]{2,1,0:T(8,128)(2,1)S(1)} %collective-permute-done.q_ref, bf16[2,2048,128]{2,1,0:T(8,128)(2,1)S(1)} %bitcast.25, bf16[2,2048,128]{2,1,0:T(8,128)(2,1)S(1)} %get-tuple-element.37.refs_2_.refs_1_, bf16[2,2048,128]{2,1,0:T(8,128)(2,1)S(1)} %bitcast.27, ...), custom_call_target="tpu_custom_call" | custom-call | flops 4831838208 | bytes 4194304 | tf_op jit(solution)/shard_map/visiting/pallas_call | solution.py:266
  15.0 0.7 %collective-permute-start.3 = (bf16[800,128]{1,0:T(8,128)(2,1)S(1)}, bf16[800,128]{1,0:T(8,128)(2,1)S(1)}, u32[]{:S(2)}, u32[]{:S(2)}) collective-permute-start(bf16[800,128]{1,0:T(8,128)(2,1)S(1)} %visiting.1), channel_id=1, source_target_pairs={{0,8},{4,12},{8,0},{12,4},{1,9},{5,13},{9,1},{13,5},{2,10},{6,14},... | collective-permute-start | bytes 614408 | tf_op jit(solution)/shard_map/ppermute | solution.py:262
  15.8 5.0 %suffix.1 = (f32[48,16,128]{2,1,0:T(8,128)S(1)}, f32[48,16,128]{2,1,0:T(8,128)S(1)}) custom-call(s32[48]{0:T(128)S(1)} %copy-done.1, s32[225]{0:T(256)S(1)} %get-tuple-element.21.item_ref, bf16[48,16,128]{2,1,0:T(8,128)(2,1)S(1)} %copy-done, bf16[48,1024,128]{2,1,0:T(8,128)(2,1)S(1)} %bitcast.20, bf16[48,1024,128]{2,1,0:T(8,128)(2,1)S(1)} %bitcast.23, ...), custom_call_target="tpu_custom_call" | custom-call | flops 402653184 | bytes 25165824 | tf_op jit(solution)/shard_map/suffix/pallas_call | solution.py:266
  20.8 1.1 %collective-permute-done.3.refs_0_ = bf16[800,128]{1,0:T(8,128)(2,1)S(1)} collective-permute-done((bf16[800,128]{1,0:T(8,128)(2,1)S(1)}, bf16[800,128]{1,0:T(8,128)(2,1)S(1)}, u32[]{:S(2)}, u32[]{:S(2)}) %collective-permute-start.3) | collective-permute-done | bytes 204832 | tf_op jit(solution)/shard_map/ppermute | solution.py:262
  21.9 0.9 %merge.1 = bf16[48,16,128]{2,1,0:T(8,128)(2,1)} custom-call(f32[48,16,128]{2,1,0:T(8,128)S(1)} %get-tuple-element.34.os_ref, f32[48,16,128]{2,1,0:T(8,128)S(1)} %get-tuple-element.35.ls_ref, bf16[800,128]{1,0:T(8,128)(2,1)S(1)} %collective-permute-done.3.refs_0_), custom_call_target="tpu_custom_call" | custom-call | tf_op jit(solution)/shard_map/merge/pallas_call | solution.py:266
  (15 shorter events, 0.0 us)
Async XLA Ops:
  0.0 7.3 %copy-start.2 = (bf16[2048,2,128]{2,1,0:T(2,128)(2,1)S(1)}, bf16[2048,2,128]{2,1,0:T(2,128)(2,1)}, u32[]{:S(2)}) copy-start(bf16[2048,2,128]{2,1,0:T(2,128)(2,1)} %param.7) | copy-start | bytes 3145732
  0.0 7.4 %copy-start.3 = (bf16[2048,2,128]{2,1,0:T(2,128)(2,1)S(1)}, bf16[2048,2,128]{2,1,0:T(2,128)(2,1)}, u32[]{:S(2)}) copy-start(bf16[2048,2,128]{2,1,0:T(2,128)(2,1)} %param.8) | copy-start | bytes 3145732
  0.0 5.2 %collective-permute-start.2 = (bf16[4096,128]{1,0:T(8,128)(2,1)}, bf16[4096,128]{1,0:T(8,128)(2,1)S(1)}, u32[]{:S(2)}, u32[]{:S(2)}) collective-permute-start(bf16[4096,128]{1,0:T(8,128)(2,1)} %bitcast.28), channel_id=1, source_target_pairs={{0,4},{4,0},{8,12},{12,8},{1,5},{5,1},{9,13},{13,9},{2,6},{6,2},{1... | collective-permute-start | bytes 3145736 | tf_op jit(solution)/shard_map/ppermute | solution.py:308
  0.5 6.8 %collective-permute-start.1 = (bf16[4096,128]{1,0:T(8,128)(2,1)}, bf16[4096,128]{1,0:T(8,128)(2,1)S(1)}, u32[]{:S(2)}, u32[]{:S(2)}) collective-permute-start(bf16[4096,128]{1,0:T(8,128)(2,1)} %bitcast.30), channel_id=1, source_target_pairs={{0,4},{4,0},{8,12},{12,8},{1,5},{5,1},{9,13},{13,9},{2,6},{6,2},{1... | collective-permute-start | bytes 3145736 | tf_op jit(solution)/shard_map/ppermute | solution.py:308
  0.5 10.3 %collective-permute-start = (bf16[48,16,128]{2,1,0:T(8,128)(2,1)}, bf16[48,16,128]{2,1,0:T(8,128)(2,1)S(1)}, u32[]{:S(2)}, u32[]{:S(2)}) collective-permute-start(bf16[48,16,128]{2,1,0:T(8,128)(2,1)} %q_ref.1), channel_id=1, source_target_pairs={{0,8},{4,12},{8,0},{12,4},{1,9},{5,13},{9,1},{13,5},{2,10},{6,14},... | collective-permute-start | bytes 589832 | tf_op jit(solution)/shard_map/ppermute | solution.py:262
  5.3 10.4 %slice-start.3 = ((s8[12582912]{0:T(1024)(128)(4,1)}), s8[4194304]{0:T(1024)(128)(4,1)S(1)}, s32[]{:S(2)}) async-start(s8[12582912]{0:T(1024)(128)(4,1)} %bitcast.21), calls=%async_computation.3 | async-start | bytes 8388608
  7.4 8.3 %slice-start.4 = ((s8[12582912]{0:T(1024)(128)(4,1)}), s8[4194304]{0:T(1024)(128)(4,1)S(1)}, s32[]{:S(2)}) async-start(s8[12582912]{0:T(1024)(128)(4,1)} %bitcast.21), calls=%async_computation.4 | async-start | bytes 8388608
  7.7 8.0 %slice-start = ((s8[12582912]{0:T(1024)(128)(4,1)}), s8[4194304]{0:T(1024)(128)(4,1)S(1)}, s32[]{:S(2)}) async-start(s8[12582912]{0:T(1024)(128)(4,1)} %bitcast.18), calls=%async_computation | async-start | bytes 8388608
  7.7 8.0 %copy-start = (bf16[48,16,128]{2,1,0:T(8,128)(2,1)S(1)}, bf16[48,16,128]{2,1,0:T(8,128)(2,1)}, u32[]{:S(2)}) copy-start(bf16[48,16,128]{2,1,0:T(8,128)(2,1)} %q_ref.1) | copy-start | bytes 589828
  7.7 8.0 %copy-start.1 = (s32[48]{0:T(128)S(1)}, s32[48]{0:T(128)}, u32[]{:S(2)}) copy-start(s32[48]{0:T(128)} %len_ref.1) | copy-start | bytes 580
  10.8 4.9 %slice-start.1 = ((s8[12582912]{0:T(1024)(128)(4,1)}), s8[4194304]{0:T(1024)(128)(4,1)S(1)}, s32[]{:S(2)}) async-start(s8[12582912]{0:T(1024)(128)(4,1)} %bitcast.18), calls=%async_computation.1 | async-start | bytes 8388608
  10.8 4.9 %slice-start.2 = ((s8[12582912]{0:T(1024)(128)(4,1)}), s8[4194304]{0:T(1024)(128)(4,1)S(1)}, s32[]{:S(2)}) async-start(s8[12582912]{0:T(1024)(128)(4,1)} %bitcast.18), calls=%async_computation.2 | async-start | bytes 8388608
  10.8 4.9 %slice-start.5 = ((s8[12582912]{0:T(1024)(128)(4,1)}), s8[4194304]{0:T(1024)(128)(4,1)S(1)}, s32[]{:S(2)}) async-start(s8[12582912]{0:T(1024)(128)(4,1)} %bitcast.21), calls=%async_computation.5 | async-start | bytes 8388608
  15.0 6.8 %collective-permute-start.3 = (bf16[800,128]{1,0:T(8,128)(2,1)S(1)}, bf16[800,128]{1,0:T(8,128)(2,1)S(1)}, u32[]{:S(2)}, u32[]{:S(2)}) collective-permute-start(bf16[800,128]{1,0:T(8,128)(2,1)S(1)} %visiting.1), channel_id=1, source_target_pairs={{0,8},{4,12},{8,0},{12,4},{1,9},{5,13},{9,1},{13,5},{2,10},{6,14},... | collective-permute-start | bytes 614408 | tf_op jit(solution)/shard_map/ppermute | solution.py:262

commit v3 on v2

--- a/solution.py
+++ b/solution.py
@@ -168,8 +168,7 @@
             found.append(scores_of(q_ref[r], k_ref[r, span, :]))
         return tuple(found)
 
-    def body(i, scores):
-        ahead = score_batch(i + 1)
+    def finish(i, scores):
         weights = []
         for t in range(batch):
             r, j, _ = part(item_ref[i * batch + t])
@@ -184,9 +183,13 @@
             o = jnp.dot(w, v_ref[r, span, :], preferred_element_type=F32)
             oi_ref[slot] = o * (1.0 / total)
             li_ref[slot] = jnp.broadcast_to(top + jnp.log2(total), (heads, d))
+
+    def body(i, scores):
+        ahead = score_batch(i + 1)
+        finish(i, scores)
         return ahead
 
-    lax.fori_loop(0, batches, body, score_batch(0))
+    finish(batches - 1, lax.fori_loop(0, batches - 1, body, score_batch(0)))
 
     def merge(r, _):
         live = (len_ref[r] + chunk - 1) // chunk
@@ -233,6 +236,11 @@
             lse = jnp.where(eye, jnp.broadcast_to(lse[:, None, :], (n, d, d)), 0.0)
             lse = jnp.sum(lse, axis=2, keepdims=True).reshape(m, 1)
             parts.append((o, jnp.broadcast_to(lse, (m, d))))
+        if len(parts) == 2:
+            (o, l), (o_far, l_far) = parts
+            share = 1.0 / (1.0 + jnp.exp2(jnp.minimum(l - l_far, 126.0)))
+            results.append((o + (o_far - o) * share).reshape(rows, group, d))
+            continue
         top = parts[0][1]
         for part in parts[1:]:
             top = jnp.maximum(top, part[1])

time: 23 us -> 22.9 us (level)
  Pallas kernels: 16.8 us -> 16.5 us
  waiting for transfers between devices: 1.08 us -> 1.32 us
    pallas_call x6, Pallas kernels: 16.8 us -> 16.5 us  [call(): pl.pallas_call(kernel, out_shape=out_shape, in_specs=specs, out_specs=out...]
    ppermute x2, waiting for transfers between devices: 1.07 us -> 1.31 us  [shift(): return lax.ppermute(x, 'ctx', [(i, (i + by) % n) for i in range(n)])]
  transfers between devices with their start and end apart: 4 -> 4, of which waited for: 1 -> 1; matrix products, arithmetic and copies ran while one was open for 2% -> 2% of each run, Pallas kernels for 51% -> 50%
where the time goes in v3:
time: 22.9 us; the launch traced here: 22.8 us
  Pallas kernels  16.5 us (72%)
  starting transfers between devices  4.14 us (18%)
  waiting for transfers between devices  1.32 us (6%)
  local copies, waits for them, and re-layouts  0.61 us (3%)
    pallas_call x6, Pallas kernels, call(): pl.pallas_call(kernel, out_shape=out_shape, in_specs=specs, out_specs=out...  16.5 us
    ppermute x2, starting transfers between devices, shift(): return lax.ppermute(x, 'ctx', [(i, (i + by) % n) for i in range(n)])  3.61 us
    ppermute x2, waiting for transfers between devices, shift(): return lax.ppermute(x, 'ctx', [(i, (i + by) % n) for i in range(n)])  1.31 us
    ppermute x2, starting transfers between devices, shards(): keys, values = [lax.ppermute(x, 'ctx', swap) for x in raw]  0.53 us
  transfers between devices with their start and end apart: 4, of which 1 were waited for; matrix products, arithmetic and copies ran while one was open for 2% of the time, Pallas kernels for 50%

profile of v3, /device:TPU:0, one launch (start us, length us, event | category | flops | bytes accessed | tf_op | source)
XLA Modules:
  0.0 22.8 jit_solution(8472180054430603279)
XLA Ops:
  0.0 0.5 %collective-permute-start.2 = (bf16[4096,128]{1,0:T(8,128)(2,1)}, bf16[4096,128]{1,0:T(8,128)(2,1)S(1)}, u32[]{:S(2)}, u32[]{:S(2)}) collective-permute-start(bf16[4096,128]{1,0:T(8,128)(2,1)} %bitcast.28), channel_id=1, source_target_pairs={{0,4},{4,0},{8,12},{12,8},{1,5},{5,1},{9,13},{13,9},{2,6},{6,2},{1... | collective-permute-start | bytes 3145736 | tf_op jit(solution)/shard_map/ppermute | solution.py:316
  0.5 0.1 collective-permute-start.1
  0.5 2.9 %collective-permute-start = (bf16[48,16,128]{2,1,0:T(8,128)(2,1)}, bf16[48,16,128]{2,1,0:T(8,128)(2,1)S(1)}, u32[]{:S(2)}, u32[]{:S(2)}) collective-permute-start(bf16[48,16,128]{2,1,0:T(8,128)(2,1)} %q_ref.1), channel_id=1, source_target_pairs={{0,8},{4,12},{8,0},{12,4},{1,9},{5,13},{9,1},{13,5},{2,10},{6,14},... | collective-permute-start | bytes 589832 | tf_op jit(solution)/shard_map/ppermute | solution.py:270
  3.5 1.7 %queries.1 = (bf16[2,384,128]{2,1,0:T(8,128)(2,1)S(1)}, s32[225]{0:T(256)S(1)}) custom-call(s32[48]{0:T(128)} %len_ref.1, bf16[48,16,128]{2,1,0:T(8,128)(2,1)} %q_ref.1), custom_call_target="tpu_custom_call" | custom-call | bytes 393216 | tf_op jit(solution)/shard_map/queries/pallas_call | solution.py:274
  5.2 0.0 collective-permute-done.2
  5.2 0.1 copy.16
  5.3 0.0 slice-start.3
  5.3 1.9 %first.1 = (bf16[2,384,2048]{2,1,0:T(8,128)(2,1)S(1)}, f32[2,384,128]{2,1,0:T(8,128)S(1)}) custom-call(bf16[2,384,128]{2,1,0:T(8,128)(2,1)S(1)} %get-tuple-element.22.q_ref, bf16[2,2048,128]{2,1,0:T(8,128)(2,1)S(1)} %bitcast.24), custom_call_target="tpu_custom_call" | custom-call | flops 3623878656 | bytes 2097152 | tf_op jit(solution)/shard_map/first/pallas_call | solution.py:274
  7.2 0.0 collective-permute-done.1
  7.3 0.1 copy.15
  7.4 0.0 slice-start.4
  7.4 0.3 %copy_bitcast_fusion = (bf16[2,2048,128]{2,1,0:T(8,128)(2,1)S(1)}, bf16[2,2048,128]{2,1,0:T(8,128)(2,1)S(1)}) fusion(bf16[2048,2,128]{2,1,0:T(2,128)(2,1)S(1)} %bitcast.31, bf16[2048,2,128]{2,1,0:T(2,128)(2,1)S(1)} %copy-done.3), kind=kLoop, calls=%fused_computation | loop fusion | bytes 4194304 | tf_op jit(solution)/shard_map/transpose | solution.py:304
  7.7 0.0 slice-start
  7.7 0.0 copy-start
  7.7 0.0 copy-start.1
  7.8 3.1 %own.1 = (f32[2,384,128]{2,1,0:T(8,128)S(1)}, f32[2,384,128]{2,1,0:T(8,128)S(1)}) custom-call(bf16[2,384,128]{2,1,0:T(8,128)(2,1)S(1)} %get-tuple-element.22.q_ref, bf16[2,2048,128]{2,1,0:T(8,128)(2,1)S(1)} %bitcast.26, bf16[2,2048,128]{2,1,0:T(8,128)(2,1)S(1)} %get-tuple-element.38.v_ref.refs_3_, bf16[2,384,2048]{2,1,0:T(8,128)(2,1)S(1)} %get-tuple-element.27.refs_0_, ...), custom_call_target="tpu_custom_call" | custom-call | flops 2415919104 | bytes 2097152 | tf_op jit(solution)/shard_map/own/pallas_call | solution.py:274
  10.8 0.0 slice-start.1
  10.8 0.0 slice-start.2
  10.8 0.0 slice-start.5
  10.9 4.2 %visiting.1 = bf16[800,128]{1,0:T(8,128)(2,1)S(1)} custom-call(bf16[48,16,128]{2,1,0:T(8,128)(2,1)S(1)} %collective-permute-done.q_ref, bf16[2,2048,128]{2,1,0:T(8,128)(2,1)S(1)} %bitcast.25, bf16[2,2048,128]{2,1,0:T(8,128)(2,1)S(1)} %get-tuple-element.37.refs_2_.refs_1_, bf16[2,2048,128]{2,1,0:T(8,128)(2,1)S(1)} %bitcast.27, ...), custom_call_target="tpu_custom_call" | custom-call | flops 4831838208 | bytes 4194304 | tf_op jit(solution)/shard_map/visiting/pallas_call | solution.py:274
  15.0 0.7 %collective-permute-start.3 = (bf16[800,128]{1,0:T(8,128)(2,1)S(1)}, bf16[800,128]{1,0:T(8,128)(2,1)S(1)}, u32[]{:S(2)}, u32[]{:S(2)}) collective-permute-start(bf16[800,128]{1,0:T(8,128)(2,1)S(1)} %visiting.1), channel_id=1, source_target_pairs={{0,8},{4,12},{8,0},{12,4},{1,9},{5,13},{9,1},{13,5},{2,10},{6,14},... | collective-permute-start | bytes 614408 | tf_op jit(solution)/shard_map/ppermute | solution.py:270
  15.8 4.8 %suffix.1 = (f32[48,16,128]{2,1,0:T(8,128)S(1)}, f32[48,16,128]{2,1,0:T(8,128)S(1)}) custom-call(s32[48]{0:T(128)S(1)} %copy-done.1, s32[225]{0:T(256)S(1)} %get-tuple-element.21.item_ref, bf16[48,16,128]{2,1,0:T(8,128)(2,1)S(1)} %copy-done, bf16[48,1024,128]{2,1,0:T(8,128)(2,1)S(1)} %bitcast.20, bf16[48,1024,128]{2,1,0:T(8,128)(2,1)S(1)} %bitcast.23, ...), custom_call_target="tpu_custom_call" | custom-call | flops 402653184 | bytes 25165824 | tf_op jit(solution)/shard_map/suffix/pallas_call | solution.py:274
  20.6 1.3 %collective-permute-done.3.refs_0_ = bf16[800,128]{1,0:T(8,128)(2,1)S(1)} collective-permute-done((bf16[800,128]{1,0:T(8,128)(2,1)S(1)}, bf16[800,128]{1,0:T(8,128)(2,1)S(1)}, u32[]{:S(2)}, u32[]{:S(2)}) %collective-permute-start.3) | collective-permute-done | bytes 204832 | tf_op jit(solution)/shard_map/ppermute | solution.py:270
  21.9 0.9 %merge.1 = bf16[48,16,128]{2,1,0:T(8,128)(2,1)} custom-call(f32[48,16,128]{2,1,0:T(8,128)S(1)} %get-tuple-element.34.os_ref, f32[48,16,128]{2,1,0:T(8,128)S(1)} %get-tuple-element.35.ls_ref, bf16[800,128]{1,0:T(8,128)(2,1)S(1)} %collective-permute-done.3.refs_0_), custom_call_target="tpu_custom_call" | custom-call | tf_op jit(solution)/shard_map/merge/pallas_call | solution.py:274
  (15 shorter events, 0.0 us)
Async XLA Ops:
  0.0 7.3 %copy-start.2 = (bf16[2048,2,128]{2,1,0:T(2,128)(2,1)S(1)}, bf16[2048,2,128]{2,1,0:T(2,128)(2,1)}, u32[]{:S(2)}) copy-start(bf16[2048,2,128]{2,1,0:T(2,128)(2,1)} %param.7) | copy-start | bytes 3145732
  0.0 7.4 %copy-start.3 = (bf16[2048,2,128]{2,1,0:T(2,128)(2,1)S(1)}, bf16[2048,2,128]{2,1,0:T(2,128)(2,1)}, u32[]{:S(2)}) copy-start(bf16[2048,2,128]{2,1,0:T(2,128)(2,1)} %param.8) | copy-start | bytes 3145732
  0.0 5.2 %collective-permute-start.2 = (bf16[4096,128]{1,0:T(8,128)(2,1)}, bf16[4096,128]{1,0:T(8,128)(2,1)S(1)}, u32[]{:S(2)}, u32[]{:S(2)}) collective-permute-start(bf16[4096,128]{1,0:T(8,128)(2,1)} %bitcast.28), channel_id=1, source_target_pairs={{0,4},{4,0},{8,12},{12,8},{1,5},{5,1},{9,13},{13,9},{2,6},{6,2},{1... | collective-permute-start | bytes 3145736 | tf_op jit(solution)/shard_map/ppermute | solution.py:316
  0.5 6.8 %collective-permute-start.1 = (bf16[4096,128]{1,0:T(8,128)(2,1)}, bf16[4096,128]{1,0:T(8,128)(2,1)S(1)}, u32[]{:S(2)}, u32[]{:S(2)}) collective-permute-start(bf16[4096,128]{1,0:T(8,128)(2,1)} %bitcast.30), channel_id=1, source_target_pairs={{0,4},{4,0},{8,12},{12,8},{1,5},{5,1},{9,13},{13,9},{2,6},{6,2},{1... | collective-permute-start | bytes 3145736 | tf_op jit(solution)/shard_map/ppermute | solution.py:316
  0.5 10.3 %collective-permute-start = (bf16[48,16,128]{2,1,0:T(8,128)(2,1)}, bf16[48,16,128]{2,1,0:T(8,128)(2,1)S(1)}, u32[]{:S(2)}, u32[]{:S(2)}) collective-permute-start(bf16[48,16,128]{2,1,0:T(8,128)(2,1)} %q_ref.1), channel_id=1, source_target_pairs={{0,8},{4,12},{8,0},{12,4},{1,9},{5,13},{9,1},{13,5},{2,10},{6,14},... | collective-permute-start | bytes 589832 | tf_op jit(solution)/shard_map/ppermute | solution.py:270
  5.3 10.4 %slice-start.3 = ((s8[12582912]{0:T(1024)(128)(4,1)}), s8[4194304]{0:T(1024)(128)(4,1)S(1)}, s32[]{:S(2)}) async-start(s8[12582912]{0:T(1024)(128)(4,1)} %bitcast.21), calls=%async_computation.3 | async-start | bytes 8388608
  7.4 8.3 %slice-start.4 = ((s8[12582912]{0:T(1024)(128)(4,1)}), s8[4194304]{0:T(1024)(128)(4,1)S(1)}, s32[]{:S(2)}) async-start(s8[12582912]{0:T(1024)(128)(4,1)} %bitcast.21), calls=%async_computation.4 | async-start | bytes 8388608
  7.7 8.0 %slice-start = ((s8[12582912]{0:T(1024)(128)(4,1)}), s8[4194304]{0:T(1024)(128)(4,1)S(1)}, s32[]{:S(2)}) async-start(s8[12582912]{0:T(1024)(128)(4,1)} %bitcast.18), calls=%async_computation | async-start | bytes 8388608
  7.7 8.0 %copy-start = (bf16[48,16,128]{2,1,0:T(8,128)(2,1)S(1)}, bf16[48,16,128]{2,1,0:T(8,128)(2,1)}, u32[]{:S(2)}) copy-start(bf16[48,16,128]{2,1,0:T(8,128)(2,1)} %q_ref.1) | copy-start | bytes 589828
  7.7 8.0 %copy-start.1 = (s32[48]{0:T(128)S(1)}, s32[48]{0:T(128)}, u32[]{:S(2)}) copy-start(s32[48]{0:T(128)} %len_ref.1) | copy-start | bytes 580
  10.8 4.9 %slice-start.1 = ((s8[12582912]{0:T(1024)(128)(4,1)}), s8[4194304]{0:T(1024)(128)(4,1)S(1)}, s32[]{:S(2)}) async-start(s8[12582912]{0:T(1024)(128)(4,1)} %bitcast.18), calls=%async_computation.1 | async-start | bytes 8388608
  10.8 4.9 %slice-start.2 = ((s8[12582912]{0:T(1024)(128)(4,1)}), s8[4194304]{0:T(1024)(128)(4,1)S(1)}, s32[]{:S(2)}) async-start(s8[12582912]{0:T(1024)(128)(4,1)} %bitcast.18), calls=%async_computation.2 | async-start | bytes 8388608
  10.8 4.9 %slice-start.5 = ((s8[12582912]{0:T(1024)(128)(4,1)}), s8[4194304]{0:T(1024)(128)(4,1)S(1)}, s32[]{:S(2)}) async-start(s8[12582912]{0:T(1024)(128)(4,1)} %bitcast.21), calls=%async_computation.5 | async-start | bytes 8388608
  15.0 6.8 %collective-permute-start.3 = (bf16[800,128]{1,0:T(8,128)(2,1)S(1)}, bf16[800,128]{1,0:T(8,128)(2,1)S(1)}, u32[]{:S(2)}, u32[]{:S(2)}) collective-permute-start(bf16[800,128]{1,0:T(8,128)(2,1)S(1)} %visiting.1), channel_id=1, source_target_pairs={{0,8},{4,12},{8,0},{12,4},{1,9},{5,13},{9,1},{13,5},{2,10},{6,14},... | collective-permute-start | bytes 614408 | tf_op jit(solution)/shard_map/ppermute | solution.py:270

commit v4 on v3

--- a/solution.py
+++ b/solution.py
@@ -284,8 +284,8 @@
 
     raw = [prefix_keys.reshape(-1, d), prefix_values.reshape(-1, d)]
     slots = span * kv_heads
-    chunk = 128 if span % 128 == 0 else span
-    batch = 16
+    chunk = 256 if span % 256 == 0 else span
+    batch = 8
     items = rows * (span // chunk)
     smem = pl.BlockSpec(memory_space=pltpu.SMEM)
     split_queries, table = call(

time: 22.9 us -> 22.9 us (level)
  waiting for transfers between devices: 1.32 us -> 0.01 us
  Pallas kernels: 16.5 us -> 17.8 us
    pallas_call x6, Pallas kernels: 16.5 us -> 17.8 us  [call(): pl.pallas_call(kernel, out_shape=out_shape, in_specs=specs, out_specs=out...]
    ppermute x2, waiting for transfers between devices: 1.31 us -> 0.01 us  [shift(): return lax.ppermute(x, 'ctx', [(i, (i + by) % n) for i in range(n)])]
  transfers between devices with their start and end apart: 4 -> 4, of which waited for: 1 -> 0; matrix products, arithmetic and copies ran while one was open for 2% -> 2% of each run, Pallas kernels for 50% -> 56%
where the time goes in v4:
time: 22.9 us
  Pallas kernels  17.8 us (78%)
  starting transfers between devices  4.23 us (18%)
  local copies, waits for them, and re-layouts  0.61 us (3%)
    pallas_call x6, Pallas kernels, call(): pl.pallas_call(kernel, out_shape=out_shape, in_specs=specs, out_specs=out...  17.8 us
    ppermute x2, starting transfers between devices, shift(): return lax.ppermute(x, 'ctx', [(i, (i + by) % n) for i in range(n)])  3.7 us
    ppermute x2, starting transfers between devices, shards(): keys, values = [lax.ppermute(x, 'ctx', swap) for x in raw]  0.53 us
  transfers between devices with their start and end apart: 4, of which 0 were waited for; matrix products, arithmetic and copies ran while one was open for 2% of the time, Pallas kernels for 56%

profile of v4, /device:TPU:0, one launch (start us, length us, event | category | flops | bytes accessed | tf_op | source)
XLA Modules:
  0.0 22.9 jit_solution(10914622871900466467)
XLA Ops:
  0.0 0.5 %collective-permute-start.2 = (bf16[4096,128]{1,0:T(8,128)(2,1)}, bf16[4096,128]{1,0:T(8,128)(2,1)S(1)}, u32[]{:S(2)}, u32[]{:S(2)}) collective-permute-start(bf16[4096,128]{1,0:T(8,128)(2,1)} %bitcast.28), channel_id=1, source_target_pairs={{0,4},{4,0},{8,12},{12,8},{1,5},{5,1},{9,13},{13,9},{2,6},{6,2},{1... | collective-permute-start | bytes 3145736 | tf_op jit(solution)/shard_map/ppermute | solution.py:316
  0.5 0.1 collective-permute-start.1
  0.5 2.9 %collective-permute-start = (bf16[48,16,128]{2,1,0:T(8,128)(2,1)}, bf16[48,16,128]{2,1,0:T(8,128)(2,1)S(1)}, u32[]{:S(2)}, u32[]{:S(2)}) collective-permute-start(bf16[48,16,128]{2,1,0:T(8,128)(2,1)} %q_ref.1), channel_id=1, source_target_pairs={{0,8},{4,12},{8,0},{12,4},{1,9},{5,13},{9,1},{13,5},{2,10},{6,14},... | collective-permute-start | bytes 589832 | tf_op jit(solution)/shard_map/ppermute | solution.py:270
  3.5 1.6 %queries.1 = (bf16[2,384,128]{2,1,0:T(8,128)(2,1)S(1)}, s32[113]{0:T(128)S(1)}) custom-call(s32[48]{0:T(128)} %len_ref.1, bf16[48,16,128]{2,1,0:T(8,128)(2,1)} %q_ref.1), custom_call_target="tpu_custom_call" | custom-call | bytes 393216 | tf_op jit(solution)/shard_map/queries/pallas_call | solution.py:274
  5.1 0.0 collective-permute-done.2
  5.1 0.1 copy.16
  5.2 0.0 slice-start.3
  5.3 1.9 %first.1 = (bf16[2,384,2048]{2,1,0:T(8,128)(2,1)S(1)}, f32[2,384,128]{2,1,0:T(8,128)S(1)}) custom-call(bf16[2,384,128]{2,1,0:T(8,128)(2,1)S(1)} %get-tuple-element.22.q_ref, bf16[2,2048,128]{2,1,0:T(8,128)(2,1)S(1)} %bitcast.24), custom_call_target="tpu_custom_call" | custom-call | flops 3623878656 | bytes 2097152 | tf_op jit(solution)/shard_map/first/pallas_call | solution.py:274
  7.2 0.0 collective-permute-done.1
  7.2 0.1 copy.15
  7.3 0.0 slice-start.4
  7.3 0.3 %copy_bitcast_fusion = (bf16[2,2048,128]{2,1,0:T(8,128)(2,1)S(1)}, bf16[2,2048,128]{2,1,0:T(8,128)(2,1)S(1)}) fusion(bf16[2048,2,128]{2,1,0:T(2,128)(2,1)S(1)} %bitcast.31, bf16[2048,2,128]{2,1,0:T(2,128)(2,1)S(1)} %copy-done.3), kind=kLoop, calls=%fused_computation | loop fusion | bytes 4194304 | tf_op jit(solution)/shard_map/transpose | solution.py:304
  7.6 0.0 slice-start
  7.6 0.0 copy-start
  7.6 0.0 copy-start.1
  7.7 3.1 %own.1 = (f32[2,384,128]{2,1,0:T(8,128)S(1)}, f32[2,384,128]{2,1,0:T(8,128)S(1)}) custom-call(bf16[2,384,128]{2,1,0:T(8,128)(2,1)S(1)} %get-tuple-element.22.q_ref, bf16[2,2048,128]{2,1,0:T(8,128)(2,1)S(1)} %bitcast.26, bf16[2,2048,128]{2,1,0:T(8,128)(2,1)S(1)} %get-tuple-element.38.v_ref.refs_3_, bf16[2,384,2048]{2,1,0:T(8,128)(2,1)S(1)} %get-tuple-element.27.refs_0_, ...), custom_call_target="tpu_custom_call" | custom-call | flops 2415919104 | bytes 2097152 | tf_op jit(solution)/shard_map/own/pallas_call | solution.py:274
  10.7 0.0 slice-start.1
  10.7 0.0 slice-start.2
  10.8 0.0 slice-start.5
  10.8 4.2 %visiting.1 = bf16[800,128]{1,0:T(8,128)(2,1)S(1)} custom-call(bf16[48,16,128]{2,1,0:T(8,128)(2,1)S(1)} %collective-permute-done.q_ref, bf16[2,2048,128]{2,1,0:T(8,128)(2,1)S(1)} %bitcast.25, bf16[2,2048,128]{2,1,0:T(8,128)(2,1)S(1)} %get-tuple-element.37.refs_2_.refs_1_, bf16[2,2048,128]{2,1,0:T(8,128)(2,1)S(1)} %bitcast.27, ...), custom_call_target="tpu_custom_call" | custom-call | flops 4831838208 | bytes 4194304 | tf_op jit(solution)/shard_map/visiting/pallas_call | solution.py:274
  14.9 0.8 %collective-permute-start.3 = (bf16[800,128]{1,0:T(8,128)(2,1)S(1)}, bf16[800,128]{1,0:T(8,128)(2,1)S(1)}, u32[]{:S(2)}, u32[]{:S(2)}) collective-permute-start(bf16[800,128]{1,0:T(8,128)(2,1)S(1)} %visiting.1), channel_id=1, source_target_pairs={{0,8},{4,12},{8,0},{12,4},{1,9},{5,13},{9,1},{13,5},{2,10},{6,14},... | collective-permute-start | bytes 614408 | tf_op jit(solution)/shard_map/ppermute | solution.py:270
  15.8 6.2 %suffix.1 = (f32[48,16,128]{2,1,0:T(8,128)S(1)}, f32[48,16,128]{2,1,0:T(8,128)S(1)}) custom-call(s32[48]{0:T(128)S(1)} %copy-done.1, s32[113]{0:T(128)S(1)} %get-tuple-element.21.item_ref, bf16[48,16,128]{2,1,0:T(8,128)(2,1)S(1)} %copy-done, bf16[48,1024,128]{2,1,0:T(8,128)(2,1)S(1)} %bitcast.20, bf16[48,1024,128]{2,1,0:T(8,128)(2,1)S(1)} %bitcast.23, ...), custom_call_target="tpu_custom_call" | custom-call | flops 402653184 | bytes 25165824 | tf_op jit(solution)/shard_map/suffix/pallas_call | solution.py:274
  22.0 0.0 collective-permute-done.3.refs_0_
  22.0 0.9 %merge.1 = bf16[48,16,128]{2,1,0:T(8,128)(2,1)} custom-call(f32[48,16,128]{2,1,0:T(8,128)S(1)} %get-tuple-element.34.os_ref, f32[48,16,128]{2,1,0:T(8,128)S(1)} %get-tuple-element.35.ls_ref, bf16[800,128]{1,0:T(8,128)(2,1)S(1)} %collective-permute-done.3.refs_0_), custom_call_target="tpu_custom_call" | custom-call | tf_op jit(solution)/shard_map/merge/pallas_call | solution.py:274
  (15 shorter events, 0.0 us)
Async XLA Ops:
  0.0 7.2 %copy-start.2 = (bf16[2048,2,128]{2,1,0:T(2,128)(2,1)S(1)}, bf16[2048,2,128]{2,1,0:T(2,128)(2,1)}, u32[]{:S(2)}) copy-start(bf16[2048,2,128]{2,1,0:T(2,128)(2,1)} %param.7) | copy-start | bytes 3145732
  0.0 7.3 %copy-start.3 = (bf16[2048,2,128]{2,1,0:T(2,128)(2,1)S(1)}, bf16[2048,2,128]{2,1,0:T(2,128)(2,1)}, u32[]{:S(2)}) copy-start(bf16[2048,2,128]{2,1,0:T(2,128)(2,1)} %param.8) | copy-start | bytes 3145732
  0.0 5.1 %collective-permute-start.2 = (bf16[4096,128]{1,0:T(8,128)(2,1)}, bf16[4096,128]{1,0:T(8,128)(2,1)S(1)}, u32[]{:S(2)}, u32[]{:S(2)}) collective-permute-start(bf16[4096,128]{1,0:T(8,128)(2,1)} %bitcast.28), channel_id=1, source_target_pairs={{0,4},{4,0},{8,12},{12,8},{1,5},{5,1},{9,13},{13,9},{2,6},{6,2},{1... | collective-permute-start | bytes 3145736 | tf_op jit(solution)/shard_map/ppermute | solution.py:316
  0.5 6.7 %collective-permute-start.1 = (bf16[4096,128]{1,0:T(8,128)(2,1)}, bf16[4096,128]{1,0:T(8,128)(2,1)S(1)}, u32[]{:S(2)}, u32[]{:S(2)}) collective-permute-start(bf16[4096,128]{1,0:T(8,128)(2,1)} %bitcast.30), channel_id=1, source_target_pairs={{0,4},{4,0},{8,12},{12,8},{1,5},{5,1},{9,13},{13,9},{2,6},{6,2},{1... | collective-permute-start | bytes 3145736 | tf_op jit(solution)/shard_map/ppermute | solution.py:316
  0.5 10.2 %collective-permute-start = (bf16[48,16,128]{2,1,0:T(8,128)(2,1)}, bf16[48,16,128]{2,1,0:T(8,128)(2,1)S(1)}, u32[]{:S(2)}, u32[]{:S(2)}) collective-permute-start(bf16[48,16,128]{2,1,0:T(8,128)(2,1)} %q_ref.1), channel_id=1, source_target_pairs={{0,8},{4,12},{8,0},{12,4},{1,9},{5,13},{9,1},{13,5},{2,10},{6,14},... | collective-permute-start | bytes 589832 | tf_op jit(solution)/shard_map/ppermute | solution.py:270
  5.2 10.5 %slice-start.3 = ((s8[12582912]{0:T(1024)(128)(4,1)}), s8[4194304]{0:T(1024)(128)(4,1)S(1)}, s32[]{:S(2)}) async-start(s8[12582912]{0:T(1024)(128)(4,1)} %bitcast.21), calls=%async_computation.3 | async-start | bytes 8388608
  7.3 8.4 %slice-start.4 = ((s8[12582912]{0:T(1024)(128)(4,1)}), s8[4194304]{0:T(1024)(128)(4,1)S(1)}, s32[]{:S(2)}) async-start(s8[12582912]{0:T(1024)(128)(4,1)} %bitcast.21), calls=%async_computation.4 | async-start | bytes 8388608
  7.6 8.1 %slice-start = ((s8[12582912]{0:T(1024)(128)(4,1)}), s8[4194304]{0:T(1024)(128)(4,1)S(1)}, s32[]{:S(2)}) async-start(s8[12582912]{0:T(1024)(128)(4,1)} %bitcast.18), calls=%async_computation | async-start | bytes 8388608
  7.6 8.1 %copy-start = (bf16[48,16,128]{2,1,0:T(8,128)(2,1)S(1)}, bf16[48,16,128]{2,1,0:T(8,128)(2,1)}, u32[]{:S(2)}) copy-start(bf16[48,16,128]{2,1,0:T(8,128)(2,1)} %q_ref.1) | copy-start | bytes 589828
  7.6 8.1 %copy-start.1 = (s32[48]{0:T(128)S(1)}, s32[48]{0:T(128)}, u32[]{:S(2)}) copy-start(s32[48]{0:T(128)} %len_ref.1) | copy-start | bytes 580
  10.7 5.0 %slice-start.1 = ((s8[12582912]{0:T(1024)(128)(4,1)}), s8[4194304]{0:T(1024)(128)(4,1)S(1)}, s32[]{:S(2)}) async-start(s8[12582912]{0:T(1024)(128)(4,1)} %bitcast.18), calls=%async_computation.1 | async-start | bytes 8388608
  10.7 5.0 %slice-start.2 = ((s8[12582912]{0:T(1024)(128)(4,1)}), s8[4194304]{0:T(1024)(128)(4,1)S(1)}, s32[]{:S(2)}) async-start(s8[12582912]{0:T(1024)(128)(4,1)} %bitcast.18), calls=%async_computation.2 | async-start | bytes 8388608
  10.8 5.0 %slice-start.5 = ((s8[12582912]{0:T(1024)(128)(4,1)}), s8[4194304]{0:T(1024)(128)(4,1)S(1)}, s32[]{:S(2)}) async-start(s8[12582912]{0:T(1024)(128)(4,1)} %bitcast.21), calls=%async_computation.5 | async-start | bytes 8388608
  14.9 7.1 %collective-permute-start.3 = (bf16[800,128]{1,0:T(8,128)(2,1)S(1)}, bf16[800,128]{1,0:T(8,128)(2,1)S(1)}, u32[]{:S(2)}, u32[]{:S(2)}) collective-permute-start(bf16[800,128]{1,0:T(8,128)(2,1)S(1)} %visiting.1), channel_id=1, source_target_pairs={{0,8},{4,12},{8,0},{12,4},{1,9},{5,13},{9,1},{13,5},{2,10},{6,14},... | collective-permute-start | bytes 614408 | tf_op jit(solution)/shard_map/ppermute | solution.py:270
